TPU v7x, 256 devices: a whole 4x4x8 slice. The times are simulated.
256 devices in a mesh: comp: 2 (over core), gx: 8 (over z_hi, x), gy: 16 (over z_lo, y).
Axes of the slice: x: 4, y: 4, z: 8 (z_hi: 2, z_lo: 4; z = z_hi * 4 + z_lo), core: 2. Of those that a mesh axis runs over, the one named last changes fastest.
Arguments:
- cotangent: float32 [2, 8, 16, 320, 1024], P('comp', 'gx', 'gy'), may hold values from -6 to 6
- metric: float32 [2, 8, 16, 64, 1024], P('comp', 'gx', 'gy'), may hold values from 0.3 to 3
- volume_ops: bfloat16 [2, 320, 320], P('comp'), may hold values from -0.3125 to 0.3125
- face_ops: float32 [2, 6, 80, 80], P('comp'), may hold values from -0.625 to 0.625
- land_mask: int32 [8, 16, 256], P('gx', 'gy'), may hold values 0 or 1
- intersection: int32 [16], replicated, may hold values from 0 to 7
Outputs:
- adjoint_state: float32 [2, 8, 16, 320, 1024], P('comp', 'gx', 'gy')
All inputs are finite; a program needn't handle non-finite values. No bound on the sum of `land_mask` on one device may be relied on, other than what follows from the above.
Results may differ from a plain program's by a relative error of at most 0.0015.
Values sent between devices are 32-bit elements; how exact they have to be, the bound alone decides.
A program may use at most 64 MiB of HBM per device.

v0:
```python
import jax
import jax.numpy as jnp
from jax import lax
from jax.sharding import PartitionSpec as P

CX = 16
CY = 16
LEV = 4


DT_STEP = 0.4
EXACT = lax.Precision.HIGHEST


def swapped(block, axis, distance):
    count = lax.axis_size(axis)
    route = []
    for low in range(count):
        high = low | 1 << distance
        if high != low and high < count:
            route += [(low, high), (high, low)]
    return lax.ppermute(block, axis, route)


def shifted(value, axis, steps):
    count = lax.axis_size(axis)
    pairs = [(source, (source + steps) % count) for source in range(count)]
    return lax.ppermute(value, axis, pairs)


def passed_along(x, axis, by):
    length = lax.axis_size(axis)
    pairs = [(i, i + by) for i in range(length) if 0 <= i + by < length]
    return lax.ppermute(x, axis, pairs)


def face_selector():
    rows = jnp.arange(480, dtype=jnp.int32)
    face_no = rows // 80
    within = rows % 80
    field_no = within // 16
    first = within // 4 % 4
    second = within % 4
    node_pos = jnp.where(face_no % 2 == 0, 0, 3)
    code = face_no // 2
    node = jnp.where(
        code == 0,
        node_pos * 16 + first * 4 + second,
        jnp.where(
            code == 1, first * 16 + node_pos * 4 + second, first * 16 + second * 4 + node_pos
        ),
    )
    target = field_no * 64 + node
    return (target[:, None] == jnp.arange(320, dtype=jnp.int32)[None, :]).astype(jnp.float32)


def column_tables():
    columns = CX * CY
    source = jnp.arange(columns, dtype=jnp.int32)[:, None]
    target = jnp.arange(columns, dtype=jnp.int32)[None, :]
    target_x = target // CY
    target_y = target % CY
    from_west = ((source == target - CY) & (target_x > 0)).astype(jnp.float32)
    from_east = ((source == target + CY) & (target_x < CX - 1)).astype(jnp.float32)
    from_south = ((source == target - 1) & (target_y > 0)).astype(jnp.float32)
    from_north = ((source == target + 1) & (target_y < CY - 1)).astype(jnp.float32)
    lat_ids = jnp.arange(CY, dtype=jnp.int32)[:, None]
    lon_ids = jnp.arange(CX, dtype=jnp.int32)[:, None]
    place_west = ((target_x == 0) & (target_y == lat_ids)).astype(jnp.float32)
    place_east = ((target_x == CX - 1) & (target_y == lat_ids)).astype(jnp.float32)
    place_south = ((target_y == 0) & (target_x == lon_ids)).astype(jnp.float32)
    place_north = ((target_y == CY - 1) & (target_x == lon_ids)).astype(jnp.float32)
    return (
        from_west,
        from_east,
        from_south,
        from_north,
        place_west,
        place_east,
        place_south,
        place_north,
    )


def column_mask(field, mask_f):
    shaped = field.reshape(320, LEV, CX * CY) * mask_f[None, None, :]
    return shaped.reshape(field.shape)


def across_sections(block):
    return swapped(block, "comp", 0)


def along_longitude(block, amount, tiles_x):
    source = (lax.axis_index("gx") - amount + tiles_x) % tiles_x
    piece = lax.all_gather(block[None], "gx", axis=0, tiled=True)
    tile_ids = jnp.arange(piece.shape[0], dtype=jnp.int32)
    chosen = (tile_ids == source).astype(jnp.float32)
    return jnp.sum(piece * chosen[:, None, None], axis=0)


def body(cotangent, metric, volume_ops, face_ops, land_mask, intersection):
    state = cotangent[0, 0, 0]
    weights = metric[0, 0, 0]
    volume = volume_ops[0]
    lifting = face_ops[0]
    section = lax.axis_index("comp")
    tiles_x = lax.axis_size("gx")
    is_air = section == 0
    mask_f = jnp.where(is_air, 1.0, land_mask[0, 0].astype(jnp.float32))
    offset = intersection[lax.axis_index("gy")]
    back_amount = (tiles_x - offset) % tiles_x
    columns = CX * CY
    flat_rows = 80 * LEV
    selector = face_selector()
    lift_matrix = jnp.einsum(
        "kim,kij->mkj", selector.reshape(6, 80, 320), lifting, precision=EXACT
    ).reshape(320, 480)
    (
        from_west,
        from_east,
        from_south,
        from_north,
        place_west,
        place_east,
        place_south,
        place_north,
    ) = column_tables()

    def couple(surface):
        return along_longitude(
            across_sections(surface), jnp.where(is_air, back_amount, offset), tiles_x
        )

    def apply_adjoint(field):
        elems = field.shape[-1]
        traces = jnp.dot(selector, field, precision=EXACT)
        layered = traces.reshape(6, 80, LEV, columns)
        flat = traces.reshape(6, flat_rows, columns)
        x_low, x_high, y_low, y_high = (flat[0], flat[1], flat[2], flat[3])
        west_src = jnp.dot(x_high, place_east.T, precision=EXACT)
        east_src = jnp.dot(x_low, place_west.T, precision=EXACT)
        south_src = jnp.dot(y_high, place_north.T, precision=EXACT)
        north_src = jnp.dot(y_low, place_south.T, precision=EXACT)
        west = shifted(west_src, "gx", 1)
        east = shifted(east_src, "gx", -1)
        south = passed_along(south_src, "gy", 1)
        north = passed_along(north_src, "gy", -1)
        z_low = layered[4]
        z_high = layered[5]
        surface = jnp.where(is_air, z_low[:, 0], z_high[:, LEV - 1])
        partner = couple(surface)
        below = jnp.where(is_air, partner, 0.0)
        above = jnp.where(is_air, 0.0, partner)
        next_x_low = jnp.dot(x_high, from_west, precision=EXACT) + jnp.dot(
            west, place_west, precision=EXACT
        )
        next_x_high = jnp.dot(x_low, from_east, precision=EXACT) + jnp.dot(
            east, place_east, precision=EXACT
        )
        next_y_low = jnp.dot(y_high, from_south, precision=EXACT) + jnp.dot(
            south, place_south, precision=EXACT
        )
        next_y_high = jnp.dot(y_low, from_north, precision=EXACT) + jnp.dot(
            north, place_north, precision=EXACT
        )
        next_z_low = jnp.concatenate([below[:, None, :], z_high[:, :-1]], axis=1)
        next_z_high = jnp.concatenate([z_low[:, 1:], above[:, None, :]], axis=1)
        planar = jnp.stack([next_x_low, next_x_high, next_y_low, next_y_high]).reshape(
            4, 80, LEV, columns
        )
        vertical = jnp.stack([next_z_low, next_z_high])
        jumps = jnp.concatenate([planar, vertical], axis=0).reshape(480, elems) - traces
        lifted = jnp.dot(lift_matrix, jumps, precision=EXACT)
        volume_term = jnp.dot(
            volume, field.astype(jnp.bfloat16), preferred_element_type=jnp.float32
        )
        result = (volume_term.reshape(5, 64, elems) * weights[None, :, :]).reshape(
            320, elems
        ) + lifted
        return column_mask(result, mask_f)

    start = column_mask(state, mask_f)
    half_state = 0.5 * start
    segment_one = half_state + DT_STEP * apply_adjoint(half_state)
    final = 0.5 * start + segment_one + DT_STEP * apply_adjoint(segment_one)
    return final[None, None, None]


def solution(mesh):
    in_specs = (
        P("comp", "gx", "gy", None, None),
        P("comp", "gx", "gy", None, None),
        P("comp", None, None),
        P("comp", None, None, None),
        P("gx", "gy", None),
        P(),
    )
    out_specs = P("comp", "gx", "gy", None, None)
    return jax.shard_map(body, mesh=mesh, in_specs=in_specs, out_specs=out_specs, check_vma=False)
```

profile of v0, /device:TPU:24, one launch (start us, length us, event | category | flops | bytes accessed | tf_op | source)
XLA Modules:
  0.0 225.6 jit_solution(17380222102938064320)
XLA Ops:
  0.8 3.1 %fusion.32 = f32[480,1024]{1,0:T(8,128)S(1)} fusion(f32[1,1,1,320,1024]{4,3,2,1,0:T(8,128)} %param.6, f32[1024]{0:T(1024)S(1)} %bitcast.119, s32[480]{0:T(512)S(1)} %fusion.174), kind=kOutput, calls=%fused_computation.28 | convolution fusion | flops 1888245760 | bytes 3282816 | tf_op jit(solution)/shard_map/dot_general | solution.py:137
  4.1 1.1 copy-done.2
  6.3 9.4 %collective-permute-start.1 = (f32[320,16]{1,0:T(8,128)}, f32[320,16]{1,0:T(8,128)}, u32[]{:S(2)}, u32[]{:S(2)}) collective-permute-start(f32[320,16]{1,0:T(8,128)} %fusion.114), channel_id=1, source_target_pairs={{0,112},{16,0},{32,16},{48,32},{64,48},{80,64},{96,80},{112,96},{1... | collective-permute-start | bytes 61448 | tf_op jit(solution)/shard_map/ppermute | solution.py:28
  17.8 2.6 %collective-permute-start.2 = (f32[320,16]{1,0:T(8,128)}, f32[320,16]{1,0:T(8,128)}, u32[]{:S(2)}, u32[]{:S(2)}) collective-permute-start(f32[320,16]{1,0:T(8,128)} %fusion.95), channel_id=1, source_target_pairs={{0,1},{1,2},{2,3},{3,4},{4,5},{5,6},{6,7},{7,8},{8,9},{9,10},{10,1... | collective-permute-start | bytes 61448 | tf_op jit(solution)/shard_map/ppermute | solution.py:34
  21.5 3.2 %collective-permute-start.3 = (f32[320,16]{1,0:T(8,128)}, f32[320,16]{1,0:T(8,128)}, u32[]{:S(2)}, u32[]{:S(2)}) collective-permute-start(f32[320,16]{1,0:T(8,128)} %fusion.100), channel_id=1, source_target_pairs={{1,0},{2,1},{3,2},{4,3},{5,4},{6,5},{7,6},{8,7},{9,8},{10,9},{11,1... | collective-permute-start | bytes 61448 | tf_op jit(solution)/shard_map/ppermute | solution.py:34
  31.6 1.1 fusion.53
  33.7 1.0 fusion.68
  34.8 2.4 %fusion.35 = f32[6,320,80]{1,2,0:T(8,128)} fusion(s32[6,80]{1,0:T(8,128)S(1)} %fusion.151, f32[1,6,80,80]{3,2,1,0:T(8,128)} %param.9), kind=kOutput, calls=%fused_computation.32 | convolution fusion | flops 147609600 | bytes 769920 | tf_op jit(solution)/shard_map/kim,kij->mkj/dot_general | solution.py:116
  38.6 2.5 %bitcast_multiply_fusion.1 = f32[320,1024]{1,0:T(8,128)} fusion(f32[1,1,1,320,1024]{4,3,2,1,0:T(8,128)S(1)} %copy-done.1, f32[64,1024]{1,0:T(8,128)} %bitcast.117, f32[1024]{0:T(1024)S(1)} %bitcast.120, bf16[1,320,320]{2,1,0:T(8,128)(2,1)S(1)} %copy-done), kind=kOutput, calls=%fused_computation.1 | convolution fusion | flops 211025920 | bytes 3092480 | tf_op jit(solution)/shard_map/dot_general | solution.py:175
  41.1 1.9 convolution_add_fusion.6
  43.0 1.2 convolution_add_fusion.7
  45.1 1.9 convolution_add_fusion.5
  48.0 1.8 stack.39
  49.8 1.8 stack.40
  51.6 2.1 convolution_add_fusion.4
  53.6 1.8 stack.41
  55.4 1.1 constant_dynamic-update-slice_fusion.2
  56.5 1.1 constant_dynamic-update-slice_fusion.1
  58.6 46.0 %all-gather = f32[640,256]{1,0:T(8,128)S(1)} all-gather(f32[80,256]{1,0:T(8,128)} %collective-permute-done.4), channel_id=2, replica_groups=mesh['comp'=2,'gx'=8,'gy'=16] {'gx'}, dimensions={0}, use_global_device_ids=true | all-gather | bytes 737280 | tf_op jit(solution)/shard_map/all_gather | solution.py:96
  108.0 2.5 %fusion.28 = f32[320,1024]{1,0:T(8,128)S(1)} fusion(f32[320,1024]{1,0:T(8,128)S(1)} %copy-done.9, f32[320,480]{0,1:T(8,128)S(1)} %bitcast.109, f32[480,1024]{1,0:T(8,128)S(1)} %bitcast.108, f32[480,1024]{1,0:T(8,128)S(1)} %copy-done.3, f32[1,1,1,320,1024]{4,3,2,1,0:T(8,128)S(1)} %copy-done.1, f32[1024]{0:T(1024)S(1)} %bitcast.121), kind=kOutput, calls=%fused_computation.14 | convolution fusion | flops 1889894400 | bytes 8482816 | tf_op jit(solution)/shard_map/dot_general | solution.py:174
  110.5 1.8 fusion.34
  112.3 1.3 fusion.192
  114.2 1.1 squeeze.62
  116.2 1.7 fusion.66
  117.9 1.1 squeeze.61
  119.9 1.6 fusion.61
  121.6 1.1 squeeze.60
  123.6 1.7 fusion.56
  125.3 1.8 squeeze.63
  127.3 2.7 %collective-permute-start.8 = (f32[320,16]{1,0:T(8,128)}, f32[320,16]{1,0:T(8,128)}, u32[]{:S(2)}, u32[]{:S(2)}) collective-permute-start(f32[320,16]{1,0:T(8,128)} %fusion.97), channel_id=1, source_target_pairs={{1,0},{2,1},{3,2},{4,3},{5,4},{6,5},{7,6},{8,7},{9,8},{10,9},{11,1... | collective-permute-start | bytes 61448 | tf_op jit(solution)/shard_map/ppermute | solution.py:34
  130.0 1.1 squeeze.59
  131.1 1.7 fusion.51
  132.8 1.1 broadcast_select_fusion
  134.8 1.1 slice.111
  136.0 1.6 bitcast_multiply_fusion
  138.2 5.3 %collective-permute-start.7 = (f32[320,16]{1,0:T(8,128)S(1)}, f32[320,16]{1,0:T(8,128)S(1)}, u32[]{:S(2)}, u32[]{:S(2)}) collective-permute-start(f32[320,16]{1,0:T(8,128)S(1)} %copy-done.19), channel_id=1, source_target_pairs={{0,1},{1,2},{2,3},{3,4},{4,5},{5,6},{6,7},{7,8},{8,9},{9,10},{10,1... | collective-permute-start | bytes 61448 | tf_op jit(solution)/shard_map/ppermute | solution.py:34
  143.5 7.7 %collective-permute-start.6 = (f32[320,16]{1,0:T(8,128)S(1)}, f32[320,16]{1,0:T(8,128)S(1)}, u32[]{:S(2)}, u32[]{:S(2)}) collective-permute-start(f32[320,16]{1,0:T(8,128)S(1)} %copy-done.18), channel_id=1, source_target_pairs={{0,112},{16,0},{32,16},{48,32},{64,48},{80,64},{96,80},{112,96},{1... | collective-permute-start | bytes 61448 | tf_op jit(solution)/shard_map/ppermute | solution.py:28
  151.2 1.9 convolution_add_fusion
  154.2 4.3 %collective-permute-done.6 = f32[320,16]{1,0:T(8,128)S(1)} collective-permute-done((f32[320,16]{1,0:T(8,128)S(1)}, f32[320,16]{1,0:T(8,128)S(1)}, u32[]{:S(2)}, u32[]{:S(2)}) %collective-permute-start.6) | collective-permute-done | bytes 20512 | tf_op jit(solution)/shard_map/ppermute | solution.py:28
  159.5 1.8 stack.47
  161.3 1.8 stack.46
  163.1 1.8 stack.45
  164.9 2.2 collective-permute-done.5
  167.1 2.1 convolution_add_fusion.3
  169.1 1.8 stack.44
  170.9 1.0 constant_dynamic-update-slice_fusion.7
  174.1 45.2 %all-gather.1 = f32[640,256]{1,0:T(8,128)S(1)} all-gather(f32[80,256]{1,0:T(8,128)} %collective-permute-done.9), channel_id=3, replica_groups=mesh['comp'=2,'gx'=8,'gy'=16] {'gx'}, dimensions={0}, use_global_device_ids=true | all-gather | bytes 737280 | tf_op jit(solution)/shard_map/all_gather | solution.py:96
  222.0 3.6 %fusion.19 = f32[1,1,1,320,1024]{4,3,2,1,0:T(8,128)} fusion(f32[320,1024]{1,0:T(8,128)S(1)} %copy-done.8, f32[320,480]{0,1:T(8,128)S(1)} %bitcast.110, f32[480,1024]{1,0:T(8,128)S(1)} %bitcast.107, f32[480,1024]{1,0:T(8,128)S(1)} %copy-done.5, f32[320,1024]{1,0:T(8,128)S(1)} %fusion.28, f32[1,1,1,320,1024]{4,3,2,1,0:T(8,128)S(1)} %copy-done.1, ...), kind=kOutput, calls=%fused_computation.11 | convolution fusion | flops 1890222080 | bytes 9793536 | tf_op jit(solution)/shard_map/dot_general | solution.py:174
  (136 shorter events, 30.9 us)
Async XLA Ops:
  0.0 38.6 %copy-start = (bf16[1,320,320]{2,1,0:T(8,128)(2,1)S(1)}, bf16[1,320,320]{2,1,0:T(8,128)(2,1)}, u32[]{:S(2)}) copy-start(bf16[1,320,320]{2,1,0:T(8,128)(2,1)} %param.8) | copy-start | bytes 614404
  4.0 1.3 copy-start.2
  6.3 34.8 %collective-permute-start.1 = (f32[320,16]{1,0:T(8,128)}, f32[320,16]{1,0:T(8,128)}, u32[]{:S(2)}, u32[]{:S(2)}) collective-permute-start(f32[320,16]{1,0:T(8,128)} %fusion.114), channel_id=1, source_target_pairs={{0,112},{16,0},{32,16},{48,32},{64,48},{80,64},{96,80},{112,96},{1... | collective-permute-start | bytes 61448 | tf_op jit(solution)/shard_map/ppermute | solution.py:28
  16.7 26.3 %collective-permute-start = (f32[320,16]{1,0:T(8,128)}, f32[320,16]{1,0:T(8,128)}, u32[]{:S(2)}, u32[]{:S(2)}) collective-permute-start(f32[320,16]{1,0:T(8,128)} %fusion.109), channel_id=1, source_target_pairs={{0,16},{16,32},{32,48},{48,64},{64,80},{80,96},{96,112},{112,0},{1... | collective-permute-start | bytes 61448 | tf_op jit(solution)/shard_map/ppermute | solution.py:28
  16.8 9.1 %copy-start.20 = (pred[256]{0:T(512)(128)(4,1)}, pred[256]{0:T(512)(128)(4,1)S(1)}, u32[]{:S(2)}) copy-start(pred[256]{0:T(512)(128)(4,1)S(1)} %broadcast_compare_fusion.5) | copy-start | bytes 772
  16.8 12.5 %copy-start.29 = (s32[16]{0:T(128)S(1)}, s32[16]{0:T(128)}, u32[]{:S(2)}) copy-start(s32[16]{0:T(128)} %param.11) | copy-start | bytes 196
  17.8 27.2 %collective-permute-start.2 = (f32[320,16]{1,0:T(8,128)}, f32[320,16]{1,0:T(8,128)}, u32[]{:S(2)}, u32[]{:S(2)}) collective-permute-start(f32[320,16]{1,0:T(8,128)} %fusion.95), channel_id=1, source_target_pairs={{0,1},{1,2},{2,3},{3,4},{4,5},{5,6},{6,7},{7,8},{8,9},{9,10},{10,1... | collective-permute-start | bytes 61448 | tf_op jit(solution)/shard_map/ppermute | solution.py:34
  21.5 30.1 %collective-permute-start.3 = (f32[320,16]{1,0:T(8,128)}, f32[320,16]{1,0:T(8,128)}, u32[]{:S(2)}, u32[]{:S(2)}) collective-permute-start(f32[320,16]{1,0:T(8,128)} %fusion.100), channel_id=1, source_target_pairs={{1,0},{2,1},{3,2},{4,3},{5,4},{6,5},{7,6},{8,7},{9,8},{10,9},{11,1... | collective-permute-start | bytes 61448 | tf_op jit(solution)/shard_map/ppermute | solution.py:34
  25.1 6.2 %copy-start.10 = (f32[80,4,256]{2,1,0:T(4,128)}, f32[80,4,256]{2,1,0:T(4,128)S(1)}, u32[]{:S(2)}) copy-start(f32[80,4,256]{2,1,0:T(4,128)S(1)} %squeeze.57) | copy-start | bytes 983044
  25.9 32.7 %collective-permute-start.4 = (f32[80,256]{1,0:T(8,128)}, f32[80,256]{1,0:T(8,128)}, u32[]{:S(2)}, u32[]{:S(2)}) collective-permute-start(f32[80,256]{1,0:T(8,128)} %bitcast.104), channel_id=1, source_target_pairs={{0,128},{128,0},{1,129},{129,1},{2,130},{130,2},{3,131},{131,3},{4... | collective-permute-start | bytes 245768 | tf_op jit(solution)/shard_map/ppermute | solution.py:22
  25.9 5.4 %copy-start.23 = (s32[256]{0:T(256)}, s32[256]{0:T(256)S(1)}, u32[]{:S(2)}) copy-start(s32[256]{0:T(256)S(1)} %iota_add_fusion.2) | copy-start | bytes 3076
  25.9 5.4 %copy-start.27 = (pred[256]{0:T(512)(128)(4,1)}, pred[256]{0:T(512)(128)(4,1)S(1)}, u32[]{:S(2)}) copy-start(pred[256]{0:T(512)(128)(4,1)S(1)} %broadcast_compare_fusion.6) | copy-start | bytes 772
  31.2 2.5 %copy-start.25 = (s32[256]{0:T(256)S(1)}, s32[256]{0:T(256)}, u32[]{:S(2)}) copy-start(s32[256]{0:T(256)} %iota_add_fusion) | copy-start | bytes 3076
  31.2 2.5 %copy-start.28 = (pred[256]{0:T(512)(128)(4,1)S(1)}, pred[256]{0:T(512)(128)(4,1)}, u32[]{:S(2)}) copy-start(pred[256]{0:T(512)(128)(4,1)} %broadcast_compare_fusion.4) | copy-start | bytes 772
  31.6 7.0 %copy-start.1 = (f32[1,1,1,320,1024]{4,3,2,1,0:T(8,128)S(1)}, f32[1,1,1,320,1024]{4,3,2,1,0:T(8,128)}, u32[]{:S(2)}) copy-start(f32[1,1,1,320,1024]{4,3,2,1,0:T(8,128)} %param.6) | copy-start | bytes 3932164
  43.0 8.5 %copy-start.21 = (pred[256]{0:T(512)(128)(4,1)S(1)}, pred[256]{0:T(512)(128)(4,1)}, u32[]{:S(2)}) copy-start(pred[256]{0:T(512)(128)(4,1)} %copy-done.20) | copy-start | bytes 772
  55.4 50.2 %copy-start.11 = (f32[80,4,256]{2,1,0:T(4,128)S(1)}, f32[80,4,256]{2,1,0:T(4,128)}, u32[]{:S(2)}) copy-start(f32[80,4,256]{2,1,0:T(4,128)} %copy-done.10) | copy-start | bytes 983044
  56.5 49.3 %copy-start.12 = (f32[80,3,256]{2,1,0:T(4,128)S(1)}, f32[80,3,256]{2,1,0:T(4,128)}, u32[]{:S(2)}) copy-start(f32[80,3,256]{2,1,0:T(4,128)} %slice.101) | copy-start | bytes 737284
  105.8 1.3 copy-start.9
  106.0 1.8 copy-start.3
  106.0 1.9 copy-start.6
  112.3 1.8 copy-start.4
  114.1 5.8 %copy-start.24 = (s32[256]{0:T(256)S(1)}, s32[256]{0:T(256)}, u32[]{:S(2)}) copy-start(s32[256]{0:T(256)} %iota_add_fusion.1) | copy-start | bytes 3076
  121.6 9.5 %copy-start.22 = (s32[256]{0:T(256)S(1)}, s32[256]{0:T(256)}, u32[]{:S(2)}) copy-start(s32[256]{0:T(256)} %iota_add_fusion.3) | copy-start | bytes 3076
  127.3 23.9 %collective-permute-start.8 = (f32[320,16]{1,0:T(8,128)}, f32[320,16]{1,0:T(8,128)}, u32[]{:S(2)}, u32[]{:S(2)}) collective-permute-start(f32[320,16]{1,0:T(8,128)} %fusion.97), channel_id=1, source_target_pairs={{1,0},{2,1},{3,2},{4,3},{5,4},{6,5},{7,6},{8,7},{9,8},{10,9},{11,1... | collective-permute-start | bytes 61448 | tf_op jit(solution)/shard_map/ppermute | solution.py:34
  131.1 4.9 %copy-start.17 = (f32[1,1,1,64,1024]{4,3,2,1,0:T(8,128)S(1)}, f32[1,1,1,64,1024]{4,3,2,1,0:T(8,128)}, u32[]{:S(2)}) copy-start(f32[1,1,1,64,1024]{4,3,2,1,0:T(8,128)} %param.7) | copy-start | bytes 786436
  134.8 3.4 %copy-start.19 = (f32[320,16]{1,0:T(8,128)S(1)}, f32[320,16]{1,0:T(8,128)}, u32[]{:S(2)}) copy-start(f32[320,16]{1,0:T(8,128)} %fusion.92) | copy-start | bytes 61444
  134.8 8.7 %copy-start.18 = (f32[320,16]{1,0:T(8,128)S(1)}, f32[320,16]{1,0:T(8,128)}, u32[]{:S(2)}) copy-start(f32[320,16]{1,0:T(8,128)} %fusion.111) | copy-start | bytes 61444
  134.8 16.4 %copy-start.15 = (f32[320,256]{1,0:T(8,128)S(1)}, f32[320,256]{1,0:T(8,128)}, u32[]{:S(2)}) copy-start(f32[320,256]{1,0:T(8,128)} %fusion.66) | copy-start | bytes 983044
  136.0 17.2 %copy-start.14 = (f32[320,256]{1,0:T(8,128)S(1)}, f32[320,256]{1,0:T(8,128)}, u32[]{:S(2)}) copy-start(f32[320,256]{1,0:T(8,128)} %fusion.61) | copy-start | bytes 983044
  136.0 22.5 %copy-start.13 = (f32[320,256]{1,0:T(8,128)S(1)}, f32[320,256]{1,0:T(8,128)}, u32[]{:S(2)}) copy-start(f32[320,256]{1,0:T(8,128)} %fusion.56) | copy-start | bytes 983044
  138.2 35.9 %collective-permute-start.9 = (f32[80,256]{1,0:T(8,128)}, f32[80,256]{1,0:T(8,128)}, u32[]{:S(2)}, u32[]{:S(2)}) collective-permute-start(f32[80,256]{1,0:T(8,128)} %bitcast.103), channel_id=1, source_target_pairs={{0,128},{128,0},{1,129},{129,1},{2,130},{130,2},{3,131},{131,3},{4... | collective-permute-start | bytes 245768 | tf_op jit(solution)/shard_map/ppermute | solution.py:22
  138.2 15.0 %collective-permute-start.7 = (f32[320,16]{1,0:T(8,128)S(1)}, f32[320,16]{1,0:T(8,128)S(1)}, u32[]{:S(2)}, u32[]{:S(2)}) collective-permute-start(f32[320,16]{1,0:T(8,128)S(1)} %copy-done.19), channel_id=1, source_target_pairs={{0,1},{1,2},{2,3},{3,4},{4,5},{5,6},{6,7},{7,8},{8,9},{9,10},{10,1... | collective-permute-start | bytes 61448 | tf_op jit(solution)/shard_map/ppermute | solution.py:34
  143.5 15.0 %collective-permute-start.6 = (f32[320,16]{1,0:T(8,128)S(1)}, f32[320,16]{1,0:T(8,128)S(1)}, u32[]{:S(2)}, u32[]{:S(2)}) collective-permute-start(f32[320,16]{1,0:T(8,128)S(1)} %copy-done.18), channel_id=1, source_target_pairs={{0,112},{16,0},{32,16},{48,32},{64,48},{80,64},{96,80},{112,96},{1... | collective-permute-start | bytes 61448 | tf_op jit(solution)/shard_map/ppermute | solution.py:28
  151.2 15.8 %collective-permute-start.5 = (f32[320,16]{1,0:T(8,128)}, f32[320,16]{1,0:T(8,128)}, u32[]{:S(2)}, u32[]{:S(2)}) collective-permute-start(f32[320,16]{1,0:T(8,128)} %fusion.106), channel_id=1, source_target_pairs={{0,16},{16,32},{32,48},{48,64},{64,80},{80,96},{96,112},{112,0},{1... | collective-permute-start | bytes 61448 | tf_op jit(solution)/shard_map/ppermute | solution.py:28
  169.1 50.2 %copy-start.26 = (f32[8]{0:T(128)S(1)}, f32[8]{0:T(128)}, u32[]{:S(2)}) copy-start(f32[8]{0:T(128)} %compare_convert_fusion) | copy-start | bytes 100
  170.9 3.1 %copy-start.16 = (f32[1,80,4,256]{3,2,1,0:T(4,128)S(1)}, f32[1,80,4,256]{3,2,1,0:T(4,128)}, u32[]{:S(2)}) copy-start(f32[1,80,4,256]{3,2,1,0:T(4,128)} %stack.47) | copy-start | bytes 983044
  219.8 1.3 copy-start.8
  220.0 1.8 copy-start.5
  220.0 1.9 copy-start.7
where the time goes:
time: 227 us; the launch traced here: 226 us
  blocking collectives  91.3 us (40%)
  matrix products  48.5 us (21%)
  local copies, waits for them, and re-layouts  38.8 us (17%)
  starting transfers between devices  30.9 us (14%)
  other arithmetic  7.66 us (3%)
  waiting for transfers between devices  6.54 us (3%)
    all_gather x2, blocking collectives, along_longitude(): piece = lax.all_gather(block[None], 'gx', axis=0, tiled=True)  91.3 us
    ppermute x4, starting transfers between devices, shifted(): return lax.ppermute(value, axis, pairs)  17.1 us
    unnamed x74, local copies, waits for them, and re-layouts  14.2 us
    ppermute x4, starting transfers between devices, passed_along(): return lax.ppermute(x, axis, pairs)  13.8 us
    another operation x8, local copies, waits for them, and re-layouts, apply_adjoint(): jnp.stack([next_x_low, next_x_high, next_y_low, next_y_high])  13.4 us
    ppermute x4, waiting for transfers between devices, shifted(): return lax.ppermute(value, axis, pairs)  6.53 us
    dot_general x2, matrix products, apply_adjoint(): lifted = jnp.dot(lift_matrix, jumps, precision=EXACT)  6.15 us
    dot_general x2, matrix products, apply_adjoint(): traces = jnp.dot(selector, field, precision=EXACT)  4.93 us
  transfers between devices with their start and end apart: 10, of which 2 were waited for; matrix products, arithmetic and copies ran while one was open for 27% of the time, Pallas kernels for 0%

commit v1 on v0

v1 whole, which is shorter than its diff:
```python
import functools

import jax
import jax.numpy as jnp
from jax import lax
from jax.experimental import pallas as pl
from jax.experimental.pallas import tpu as pltpu
from jax.sharding import PartitionSpec as P

MESH = pl.DeviceIdType.MESH
F32 = jnp.float32
BF16 = jnp.bfloat16
ROWS = 320
COLS = 256
LEV = 4
FACE = 80
SLOT = 256
STEP = 0.4


def iota(shape, axis):
    return lax.broadcasted_iota(jnp.int32, shape, axis)


def split3(x):
    high = x.astype(BF16)
    low = (x - high.astype(F32)).astype(BF16)
    return jnp.concatenate([high, low, high, jnp.zeros((16, x.shape[1]), BF16)], axis=0)


def a_trace(v, pos):
    n = v.shape[-1]
    return v.reshape(5, 64, n)[:, 48 * pos : 48 * pos + 16].reshape(FACE, n)


def b_trace(v, pos):
    n = v.shape[-1]
    tiles = v.reshape(10, 2, 2, 8, n)
    even = tiles[:, 0, pos].reshape(FACE, n)
    odd = tiles[:, 1, pos].reshape(FACE, n)
    lower = iota((FACE, n), 0) % 8 < 4
    if pos == 0:
        return jnp.where(lower, even, pltpu.roll(odd, 4, 0))
    return jnp.where(lower, pltpu.roll(even, FACE - 4, 0), odd)


def c_trace(ref, pos, layer):
    rows = pl.ds(3 * pos, FACE, stride=4)
    return jnp.concatenate([ref[2 * layer, rows, :], ref[2 * layer + 1, rows, :]], axis=1)


def get(ref, layer):
    return jnp.concatenate([ref[2 * layer], ref[2 * layer + 1]], axis=1)


def put(ref, layer, value):
    ref[2 * layer] = value[:, 0:128]
    ref[2 * layer + 1] = value[:, 128:256]


def placement(face):
    row = iota((ROWS, FACE), 0)
    col = iota((ROWS, FACE), 1)
    field, first, second = col // 16, col // 4 % 4, col % 4
    pos = 3 * (face % 2)
    if face // 2 == 0:
        node = pos * 16 + first * 4 + second
    elif face // 2 == 1:
        node = first * 16 + pos * 4 + second
    else:
        node = first * 16 + second * 4 + pos
    return (row == field * 64 + node).astype(BF16)


def layer_lanes(layer):
    return pl.ds(pl.multiple_of(layer * COLS, COLS), COLS)


def kernel(
    inter_hbm, cot_hbm, metric_hbm, volume_hbm, face_hbm, mask_hbm, out_hbm,
    inter, start, metric, volume, faces, mask_i,
    w, acc, lift, small, j3, face_out, face_in,
    rim_out, rim_in, s1, r1_first, r1_second, s2, r2_first, r2_second,
    local_sem, send_sem, recv_sem,
):
    c = lax.axis_index("comp")
    g = lax.axis_index("gx")
    y = lax.axis_index("gy")
    z, x = g // 4, g % 4
    last_y = lax.axis_size("gy") - 1
    other = 1 - c

    def place(comp, zz, xx):
        return {"comp": comp, "gx": zz * 4 + xx % 4, "gy": y}

    phase1 = [place(other, z, x + q) for q in range(4)]
    phase2 = [(zf, d, place(c, (z + zf) % 2, x + d)) for zf in range(2) for d in range(4) if zf or d]
    north = {"comp": c, "gx": g, "gy": jnp.minimum(y + 1, last_y)}
    south = {"comp": c, "gx": g, "gy": jnp.maximum(y - 1, 0)}

    barrier = pltpu.get_barrier_semaphore()
    for device in phase1 + [d for _, _, d in phase2]:
        pl.semaphore_signal(barrier, inc=1, device_id=device, device_id_type=MESH)

    @pl.when(y < last_y)
    def _():
        pl.semaphore_signal(barrier, inc=1, device_id=north, device_id_type=MESH)

    @pl.when(y > 0)
    def _():
        pl.semaphore_signal(barrier, inc=1, device_id=south, device_id_type=MESH)

    loads = [
        pltpu.make_async_copy(src, dst, local_sem.at[i])
        for i, (src, dst) in enumerate(
            [(cot_hbm.at[:, 128 * t : 128 * t + 128], start.at[t]) for t in range(8)]
            + [
                (mask_hbm, mask_i),
                (face_hbm, faces),
                (volume_hbm, volume),
                (metric_hbm, metric),
                (inter_hbm, inter),
            ]
        )
    ]
    for load in loads:
        load.start()

    surface = 3 * c
    r1, r2 = (r1_first, r1_second), (r2_first, r2_second)
    lane = iota((FACE, 128), 1)
    j3[...] = jnp.zeros_like(j3)

    for load in loads[0:9]:
        load.wait()
    mask = jnp.where(c == 0, 1.0, mask_i[...].astype(F32))

    def mask_start(layer, carry):
        put(start, layer, get(start, layer) * mask)
        return carry

    lax.fori_loop(0, LEV, mask_start, 0)

    def surface_trace(ref):
        return jnp.where(c == 0, c_trace(ref, 0, surface), c_trace(ref, 1, surface))

    def pack_block(block, dst):
        for q in range(4):
            dst[q, 0:40] = block[40 * (q % 2) : 40 * (q % 2) + 40, 128 * (q // 2) : 128 * (q // 2) + 128]

    def pack_rims(ref, dst):
        east = west = far = near = jnp.zeros((FACE, 128), F32)
        for layer in range(LEV):
            for half in range(2):
                v = ref[2 * layer + half]
                here = lane // 16 == layer
                if half == 1:
                    east = jnp.where(here, pltpu.roll(a_trace(v, 1), (16 * layer + 16) % 128, 1), east)
                else:
                    west = jnp.where(here, pltpu.roll(a_trace(v, 0), 16 * layer, 1), west)
                there = lane % 16 == layer + 4 * half
                far = jnp.where(there, pltpu.roll(b_trace(v, 1), (layer + 4 * half + 113) % 128, 1), far)
                near = jnp.where(there, pltpu.roll(b_trace(v, 0), layer + 4 * half, 1), near)
        dst[0], dst[1], dst[2], dst[3] = east, west, far, near

    count = [0]

    def remote(src, dst, device):
        k = count[0]
        count[0] += 1
        return pltpu.make_async_remote_copy(
            src_ref=src, dst_ref=dst, send_sem=send_sem.at[k], recv_sem=recv_sem.at[k],
            device_id=device, device_id_type=MESH,
        )

    pack_block(surface_trace(start), s1.at[0])
    pack_rims(start, rim_out.at[0])

    loads[9].wait()
    row = iota((FACE, SLOT), 0)
    col = iota((FACE, SLOT), 1)
    to_high = ((col == row) | (col == row + FACE)).astype(BF16)
    to_low = (col == row + 2 * FACE).astype(BF16)
    for face in range(6):
        scaled = STEP * faces[face]
        high = scaled.astype(BF16)
        low = (scaled - high.astype(F32)).astype(BF16)
        spread = jnp.dot(high, to_high, preferred_element_type=F32) + jnp.dot(
            low, to_low, preferred_element_type=F32
        )
        small[face] = spread.astype(BF16)
        lift[:, face * SLOT : face * SLOT + SLOT] = jnp.dot(
            placement(face), small[face], preferred_element_type=F32
        ).astype(BF16)
    face_out[...] = small[4 + c].astype(F32)

    loads[10].wait()
    loads[11].wait()
    loads[12].wait()

    off = inter[y]
    delta = jnp.where(c == 0, off, 8 - off) % 8
    shift = delta % 4
    z_from = (g + delta) % 8 // 4
    z_pick = jnp.where(z_from == z, 0, 1)

    pl.semaphore_wait(
        barrier, 11 + jnp.where(y < last_y, 1, 0) + jnp.where(y > 0, 1, 0)
    )

    swap_face = remote(face_out, face_in, phase1[0])
    piece = (40, 48)
    copies1, copies2, rims = [], [], []
    for m in range(2):
        part = pl.ds(0, piece[m])
        copies1.append([remote(s1.at[m, q, part], r1[m].at[q, part], phase1[q]) for q in range(4)])
        copies2.append([remote(s2.at[m, d, part], r2[m].at[zf, d, part], dev) for zf, d, dev in phase2])
        rims.append([
            remote(rim_out.at[m, 0], rim_in.at[m, 0], {"comp": c, "gx": (g + 1) % 8, "gy": y}),
            remote(rim_out.at[m, 1], rim_in.at[m, 1], {"comp": c, "gx": (g + 7) % 8, "gy": y}),
            remote(rim_out.at[m, 2], rim_in.at[m, 2], north),
            remote(rim_out.at[m, 3], rim_in.at[m, 3], south),
        ])

    def start_rims(m):
        rims[m][0].start()
        rims[m][1].start()

        @pl.when(y < last_y)
        def _():
            rims[m][2].start()

        @pl.when(y > 0)
        def _():
            rims[m][3].start()

    def wait_rims(m):
        rims[m][0].wait_recv()
        rims[m][1].wait_recv()

        @pl.when(y > 0)
        def _():
            rims[m][2].wait_recv()

        @pl.when(y == 0)
        def _():
            rim_in[m, 2] = jnp.zeros((FACE, 128), F32)

        @pl.when(y < last_y)
        def _():
            rims[m][3].wait_recv()

        @pl.when(y == last_y)
        def _():
            rim_in[m, 3] = jnp.zeros((FACE, 128), F32)

    def forward(m):
        for copy in copies1[m]:
            copy.wait_recv()
        for d in range(4):
            s2[m, d, 0 : piece[m]] = r1[m][(8 - d - shift) % 4, 0 : piece[m]]
        for copy in copies2[m]:
            copy.start()
        r2[m][0, 0, 0 : piece[m]] = s2[m, 0, 0 : piece[m]]

    def collect(m):
        for copy in copies2[m]:
            copy.wait_recv()
        q = [r2[m][z_pick, (8 - i - shift) % 4, 0 : piece[m]] for i in range(4)]
        left = jnp.concatenate([q[0][0:40], q[1][0:40]], axis=0)
        right = jnp.concatenate([q[2][0:40], q[3][0:40]], axis=0)
        wet = None if m == 0 else jnp.concatenate([q[0][40:41], q[2][40:41]], axis=1)
        return jnp.concatenate([left, right], axis=1), wet

    start_rims(0)
    for copy in copies1[0]:
        copy.start()
    swap_face.start()

    wide = iota((FACE, COLS), 1)

    def local(src, layer):
        lanes = layer_lanes(layer)
        v = get(src, layer)
        j3[0:SLOT] = split3(
            jnp.where(wide < 16, 0.0, pltpu.roll(a_trace(v, 1), 16, 1)) - a_trace(v, 0)
        )
        j3[SLOT : 2 * SLOT] = split3(
            jnp.where(wide >= 240, 0.0, pltpu.roll(a_trace(v, 0), 240, 1)) - a_trace(v, 1)
        )
        low, high = b_trace(v, 0), b_trace(v, 1)
        j3[2 * SLOT : 3 * SLOT] = split3(jnp.where(wide % 16 == 0, 0.0, pltpu.roll(high, 1, 1)) - low)
        j3[3 * SLOT : 4 * SLOT] = split3(jnp.where(wide % 16 == 15, 0.0, pltpu.roll(low, 255, 1)) - high)
        below = c_trace(src, 1, jnp.maximum(layer - 1, 0))
        above = c_trace(src, 0, jnp.minimum(layer + 1, LEV - 1))
        j3[4 * SLOT : 5 * SLOT] = split3(jnp.where(layer > 0, below, 0.0) - c_trace(src, 0, layer))
        j3[5 * SLOT :] = split3(jnp.where(layer < LEV - 1, above, 0.0) - c_trace(src, 1, layer))
        lifted = jnp.dot(lift[...], j3[...], preferred_element_type=F32)
        term = jnp.dot(volume[...], v.astype(BF16), preferred_element_type=F32)
        weight = STEP * metric[:, lanes]
        term = (term.reshape(5, 64, COLS) * weight[None]).reshape(ROWS, COLS)
        return (term + lifted) * mask

    def rim_part(m, layer):
        packed = [rim_in[m, k] for k in range(4)]
        west = jnp.where(lane < 16, pltpu.roll(packed[0], (128 - 16 * layer) % 128, 1), 0.0)
        east = jnp.where(lane >= 112, pltpu.roll(packed[1], 112 - 16 * layer, 1), 0.0)
        none = jnp.zeros((FACE, 128), F32)
        near, far = [], []
        for half in range(2):
            step = layer + 4 * half
            near.append(jnp.where(lane % 16 == 0, pltpu.roll(packed[2], (128 - step) % 128, 1), 0.0))
            far.append(jnp.where(lane % 16 == 15, pltpu.roll(packed[3], (143 - step) % 128, 1), 0.0))
        j3[0:SLOT] = split3(jnp.concatenate([west, none], axis=1))
        j3[SLOT : 2 * SLOT] = split3(jnp.concatenate([none, east], axis=1))
        j3[2 * SLOT : 3 * SLOT] = split3(jnp.concatenate(near, axis=1))
        j3[3 * SLOT : 4 * SLOT] = split3(jnp.concatenate(far, axis=1))
        return jnp.dot(
            lift[:, 0 : 4 * SLOT], j3[0 : 4 * SLOT], preferred_element_type=F32
        ) * mask

    def interface_part(block):
        op = lift[:, pl.ds(pl.multiple_of((4 + c) * SLOT, SLOT), SLOT)]
        return jnp.dot(op, split3(block), preferred_element_type=F32) * mask

    def first(layer, carry):
        put(w, layer, get(start, layer) + local(start, layer))
        return carry

    lax.fori_loop(0, LEV, first, 0)
    forward(0)
    wait_rims(0)

    def first_rims(layer, carry):
        put(w, layer, get(w, layer) + rim_part(0, layer))
        return carry

    lax.fori_loop(0, LEV, first_rims, 0)

    held = surface_trace(w)
    pack_block(held, s1.at[1])
    for q in range(4):
        s1[1, q, 40:48] = jnp.broadcast_to(mask[:, 128 * (q // 2) : 128 * (q // 2) + 128], (8, 128))
    for copy in copies1[1]:
        copy.start()
    swap_face.wait_recv()
    own = surface_trace(start)
    reply = jnp.dot(face_in[...].astype(BF16), split3(own), preferred_element_type=F32)
    forward(1)

    block, _ = collect(0)
    put(w, surface, get(w, surface) + interface_part(block))

    pack_rims(w, rim_out.at[1])
    start_rims(1)

    def second(layer, carry):
        put(acc, layer, get(start, layer) + get(w, layer) + local(w, layer))
        return carry

    lax.fori_loop(0, LEV, second, 0)
    wait_rims(1)

    def second_rims(layer, carry):
        put(acc, layer, 0.5 * (get(acc, layer) + rim_part(1, layer)))
        return carry

    lax.fori_loop(0, LEV, second_rims, 0)
    block, wet = collect(1)
    put(acc, surface, get(acc, surface) + 0.5 * interface_part(block + wet * reply))

    stores = [
        pltpu.make_async_copy(acc.at[t], out_hbm.at[:, 128 * t : 128 * t + 128], local_sem.at[13 + t])
        for t in range(8)
    ]
    for store in stores:
        store.start()
    for copies in [[swap_face]] + copies1 + copies2:
        for copy in copies:
            copy.wait_send()
    for m in range(2):
        rims[m][0].wait_send()
        rims[m][1].wait_send()

        @pl.when(y < last_y)
        def _():
            rims[m][2].wait_send()

        @pl.when(y > 0)
        def _():
            rims[m][3].wait_send()

    for store in stores:
        store.wait()


def body(cotangent, metric, volume_ops, face_ops, land_mask, intersection):
    copies = 31
    out = pl.pallas_call(
        kernel,
        out_shape=jax.ShapeDtypeStruct((ROWS, LEV * COLS), F32),
        in_specs=[pl.BlockSpec(memory_space=pl.ANY)] * 6,
        out_specs=pl.BlockSpec(memory_space=pl.ANY),
        scratch_shapes=[
            pltpu.SMEM((16,), jnp.int32),
            pltpu.VMEM((2 * LEV, ROWS, 128), F32),
            pltpu.VMEM((64, LEV * COLS), F32),
            pltpu.VMEM((ROWS, ROWS), BF16),
            pltpu.VMEM((6, FACE, FACE), F32),
            pltpu.VMEM((1, COLS), jnp.int32),
            pltpu.VMEM((2 * LEV, ROWS, 128), F32),
            pltpu.VMEM((2 * LEV, ROWS, 128), F32),
            pltpu.VMEM((ROWS, 6 * SLOT), BF16),
            pltpu.VMEM((6, FACE, SLOT), BF16),
            pltpu.VMEM((6 * SLOT, COLS), BF16),
            pltpu.VMEM((FACE, SLOT), F32),
            pltpu.VMEM((FACE, SLOT), F32),
            pltpu.VMEM((2, 4, FACE, 128), F32),
            pltpu.VMEM((2, 4, FACE, 128), F32),
            pltpu.VMEM((2, 4, 48, 128), F32),
            pltpu.VMEM((4, 40, 128), F32),
            pltpu.VMEM((4, 48, 128), F32),
            pltpu.VMEM((2, 4, 48, 128), F32),
            pltpu.VMEM((2, 4, 40, 128), F32),
            pltpu.VMEM((2, 4, 48, 128), F32),
            pltpu.SemaphoreType.DMA((21,)),
            pltpu.SemaphoreType.DMA((copies,)),
            pltpu.SemaphoreType.DMA((copies,)),
        ],
        compiler_params=pltpu.CompilerParams(
            collective_id=0, has_side_effects=True, vmem_limit_bytes=48 * 1024 * 1024
        ),
    )(
        intersection,
        cotangent[0, 0, 0],
        metric[0, 0, 0],
        volume_ops[0],
        face_ops[0],
        land_mask[0],
    )
    return out[None, None, None]


def solution(mesh):
    in_specs = (
        P("comp", "gx", "gy", None, None),
        P("comp", "gx", "gy", None, None),
        P("comp", None, None),
        P("comp", None, None, None),
        P("gx", "gy", None),
        P(),
    )
    out_specs = P("comp", "gx", "gy", None, None)
    return jax.shard_map(body, mesh=mesh, in_specs=in_specs, out_specs=out_specs, check_vma=False)
```

time: 227 us -> 39.8 us (0.18)
  the two profiles are of different devices: /device:TPU:24 before, /device:TPU:25 now
where the time goes in v1:
time: 39.8 us; the launch traced here: 39.6 us
  Pallas kernels  33 us (83%)
  local copies, waits for them, and re-layouts  6.54 us (16%)
    pallas_call x1, Pallas kernels, body(): pl.pallas_call(kernel, out_shape=jax.ShapeDtypeStruct((ROWS, LEV * COLS),...  33 us
    unnamed x13, local copies, waits for them, and re-layouts  6.54 us

profile of v1, /device:TPU:25, one launch (start us, length us, event | category | flops | bytes accessed | tf_op | source)
XLA Modules:
  0.0 39.6 jit_solution(174847433794111818)
XLA Ops:
  0.0 0.0 copy-start
  0.0 1.3 %copy-done = f32[1,1,1,320,1024]{4,3,2,1,0:T(8,128)S(1)} copy-done((f32[1,1,1,320,1024]{4,3,2,1,0:T(8,128)S(1)}, f32[1,1,1,320,1024]{4,3,2,1,0:T(8,128)}, u32[]{:S(2)}) %copy-start) | copy-done | bytes 1310744
  1.3 0.0 copy-start.1
  1.3 0.9 %copy-done.1 = f32[1,1,1,64,1024]{4,3,2,1,0:T(8,128)S(1)} copy-done((f32[1,1,1,64,1024]{4,3,2,1,0:T(8,128)S(1)}, f32[1,1,1,64,1024]{4,3,2,1,0:T(8,128)}, u32[]{:S(2)}) %copy-start.1) | copy-done | bytes 262168
  2.3 0.0 copy-start.2
  2.3 0.9 %copy-done.2 = bf16[1,320,320]{2,1,0:T(8,128)(2,1)S(1)} copy-done((bf16[1,320,320]{2,1,0:T(8,128)(2,1)S(1)}, bf16[1,320,320]{2,1,0:T(8,128)(2,1)}, u32[]{:S(2)}) %copy-start.2) | copy-done | bytes 204824
  3.2 0.0 copy-start.3
  3.2 0.9 %copy-done.3 = f32[1,6,80,80]{3,2,1,0:T(8,128)S(1)} copy-done((f32[1,6,80,80]{3,2,1,0:T(8,128)S(1)}, f32[1,6,80,80]{3,2,1,0:T(8,128)}, u32[]{:S(2)}) %copy-start.3) | copy-done | bytes 153624
  4.2 0.0 copy-start.4
  4.2 0.7 %copy-done.4 = s32[1,1,256]{2,1,0:T(1,128)S(1)} copy-done((s32[1,1,256]{2,1,0:T(1,128)S(1)}, s32[1,1,256]{2,1,0:T(1,128)}, u32[]{:S(2)}) %copy-start.4) | copy-done | bytes 1048
  4.8 0.0 copy-start.5
  4.8 0.7 %copy-done.5 = s32[16]{0:T(128)S(1)} copy-done((s32[16]{0:T(128)S(1)}, s32[16]{0:T(128)}, u32[]{:S(2)}) %copy-start.5) | copy-done | bytes 88
  5.5 33.0 %shard_map.64 = f32[320,1024]{1,0:T(8,128)S(1)} custom-call(s32[16]{0:T(128)S(1)} %copy-done.5, f32[320,1024]{1,0:T(8,128)S(1)} %bitcast.7, f32[64,1024]{1,0:T(8,128)S(1)} %bitcast.8, bf16[320,320]{1,0:T(8,128)(2,1)S(1)} %bitcast.9, f32[6,80,80]{2,1,0:T(8,128)S(1)} %bitcast.10, s32[1,256]{1,0:T(1,128)S(1)} %bitcast.11), custom_call_target="tpu_custom_call" | custom-call | tf_op jit(solution)/shard_map/pallas_call | solution.py:399
  38.5 1.1 %copy.8 = f32[1,1,1,320,1024]{4,3,2,1,0:T(8,128)} copy(f32[1,1,1,320,1024]{4,3,2,1,0:T(8,128)S(1)} %bitcast.6) | data formatting | bytes 2621440
Async XLA Ops:
  0.0 1.3 %copy-start = (f32[1,1,1,320,1024]{4,3,2,1,0:T(8,128)S(1)}, f32[1,1,1,320,1024]{4,3,2,1,0:T(8,128)}, u32[]{:S(2)}) copy-start(f32[1,1,1,320,1024]{4,3,2,1,0:T(8,128)} %param.6) | copy-start | bytes 3932164
  1.3 0.9 %copy-start.1 = (f32[1,1,1,64,1024]{4,3,2,1,0:T(8,128)S(1)}, f32[1,1,1,64,1024]{4,3,2,1,0:T(8,128)}, u32[]{:S(2)}) copy-start(f32[1,1,1,64,1024]{4,3,2,1,0:T(8,128)} %param.7) | copy-start | bytes 786436
  2.3 0.9 %copy-start.2 = (bf16[1,320,320]{2,1,0:T(8,128)(2,1)S(1)}, bf16[1,320,320]{2,1,0:T(8,128)(2,1)}, u32[]{:S(2)}) copy-start(bf16[1,320,320]{2,1,0:T(8,128)(2,1)} %param.8) | copy-start | bytes 614404
  3.2 0.9 %copy-start.3 = (f32[1,6,80,80]{3,2,1,0:T(8,128)S(1)}, f32[1,6,80,80]{3,2,1,0:T(8,128)}, u32[]{:S(2)}) copy-start(f32[1,6,80,80]{3,2,1,0:T(8,128)} %param.9) | copy-start | bytes 460804
  4.2 0.7 %copy-start.4 = (s32[1,1,256]{2,1,0:T(1,128)S(1)}, s32[1,1,256]{2,1,0:T(1,128)}, u32[]{:S(2)}) copy-start(s32[1,1,256]{2,1,0:T(1,128)} %param.10) | copy-start | bytes 3076
  4.8 0.7 %copy-start.5 = (s32[16]{0:T(128)S(1)}, s32[16]{0:T(128)}, u32[]{:S(2)}) copy-start(s32[16]{0:T(128)} %inter_hbm.1) | copy-start | bytes 196

commit v2 on v1

--- a/solution.py
+++ b/solution.py
@@ -72,16 +72,60 @@
     return (row == field * 64 + node).astype(BF16)
 
 
+def fold_x(v):
+    lane = iota((8, 128), 1)
+    out = [jnp.zeros((8, 128), F32)] * 2
+    for r in range(10):
+        j = r % 8
+        out[r // 8] = jnp.where(lane // 16 == j, pltpu.roll(v[8 * r : 8 * r + 8], 16 * j, 1), out[r // 8])
+    return jnp.concatenate(out, axis=0)
+
+
+def unfold_x(v):
+    tiles = []
+    for r in range(10):
+        part = v[r // 8 * 8 : r // 8 * 8 + 8]
+        tiles.append(pltpu.roll(part, (128 - 16 * (r % 8)) % 128, 1))
+    return jnp.concatenate(tiles, axis=0)
+
+
+def fold_y(v):
+    lane = iota((8, 128), 1)
+    out = [jnp.zeros((8, 128), F32)] * 2
+    for r in range(10):
+        j = r % 8
+        out[r // 8] = jnp.where(lane % 16 // 2 == j, pltpu.roll(v[8 * r : 8 * r + 8], 2 * j, 1), out[r // 8])
+    return jnp.concatenate(out, axis=0)
+
+
+def unfold_y(v):
+    tiles = []
+    for r in range(10):
+        part = v[r // 8 * 8 : r // 8 * 8 + 8]
+        tiles.append(pltpu.roll(part, (128 - 2 * (r % 8)) % 128, 1))
+    return jnp.concatenate(tiles, axis=0)
+
+
+def fold_half(v, by):
+    lane = iota((40, 128), 1)
+    return jnp.where(lane % (2 * by) < by, v[0:40], pltpu.roll(v[40:80], by, 1))
+
+
+def unfold_half(v, by):
+    return jnp.concatenate([v, pltpu.roll(v, 128 - by, 1)], axis=0)
+
+
 def layer_lanes(layer):
     return pl.ds(pl.multiple_of(layer * COLS, COLS), COLS)
 
 
 def kernel(
-    inter_hbm, cot_hbm, metric_hbm, volume_hbm, face_hbm, mask_hbm, out_hbm,
+    inter_hbm, cot_hbm, metric_hbm, volume_hbm, face_hbm, mask_hbm, acc,
     inter, start, metric, volume, faces, mask_i,
-    w, acc, lift, small, j3, face_out, face_in,
-    rim_out, rim_in, s1, r1_first, r1_second, s2, r2_first, r2_second,
-    local_sem, send_sem, recv_sem,
+    w, lift, small, j3, face_out, face_in,
+    rim_out, rim_in, s1, r1, s2, r2, ua_out, ua_in, ub_out, ub_in,
+    patch_rows, patch_out, patch_in, side_out, side_in, edge_out, edge_in, rim_edge, rim_full,
+    local_sem, send_sem, recv_sem, side_sem,
 ):
     c = lax.axis_index("comp")
     g = lax.axis_index("gx")
@@ -93,13 +137,14 @@
     def place(comp, zz, xx):
         return {"comp": comp, "gx": zz * 4 + xx % 4, "gy": y}
 
+    mates = [(zf, d, place(other, (z + zf) % 2, x + d)) for zf in range(2) for d in range(4)]
     phase1 = [place(other, z, x + q) for q in range(4)]
     phase2 = [(zf, d, place(c, (z + zf) % 2, x + d)) for zf in range(2) for d in range(4) if zf or d]
     north = {"comp": c, "gx": g, "gy": jnp.minimum(y + 1, last_y)}
     south = {"comp": c, "gx": g, "gy": jnp.maximum(y - 1, 0)}
 
     barrier = pltpu.get_barrier_semaphore()
-    for device in phase1 + [d for _, _, d in phase2]:
+    for device in [d for _, _, d in mates + phase2]:
         pl.semaphore_signal(barrier, inc=1, device_id=device, device_id_type=MESH)
 
     @pl.when(y < last_y)
@@ -127,7 +172,6 @@
         load.start()
 
     surface = 3 * c
-    r1, r2 = (r1_first, r1_second), (r2_first, r2_second)
     lane = iota((FACE, 128), 1)
     j3[...] = jnp.zeros_like(j3)
 
@@ -161,7 +205,8 @@
                 there = lane % 16 == layer + 4 * half
                 far = jnp.where(there, pltpu.roll(b_trace(v, 1), (layer + 4 * half + 113) % 128, 1), far)
                 near = jnp.where(there, pltpu.roll(b_trace(v, 0), layer + 4 * half, 1), near)
-        dst[0], dst[1], dst[2], dst[3] = east, west, far, near
+        dst[0, 0:40], dst[1, 0:40] = fold_half(east, 64), fold_half(west, 64)
+        dst[2, 0:40], dst[3, 0:40] = fold_half(far, 8), fold_half(near, 8)
 
     count = [0]
 
@@ -173,8 +218,13 @@
             device_id=device, device_id_type=MESH,
         )
 
-    pack_block(surface_trace(start), s1.at[0])
+    own = surface_trace(start)
+    pack_block(own, s1)
     pack_rims(start, rim_out.at[0])
+    rim_out[0, 0, 40:48] = jnp.broadcast_to(pltpu.roll(mask[:, 128:256], 16, 1), (8, 128))
+    rim_out[0, 1, 40:48] = jnp.broadcast_to(mask[:, 0:128], (8, 128))
+    side_out[0] = fold_x(pltpu.roll(own[:, 128:256], 16, 1))
+    side_out[1] = fold_x(own[:, 0:128])
 
     loads[9].wait()
     row = iota((FACE, SLOT), 0)
@@ -204,78 +254,87 @@
     z_from = (g + delta) % 8 // 4
     z_pick = jnp.where(z_from == z, 0, 1)
 
-    pl.semaphore_wait(
-        barrier, 11 + jnp.where(y < last_y, 1, 0) + jnp.where(y > 0, 1, 0)
-    )
-
-    swap_face = remote(face_out, face_in, phase1[0])
-    piece = (40, 48)
-    copies1, copies2, rims = [], [], []
-    for m in range(2):
-        part = pl.ds(0, piece[m])
-        copies1.append([remote(s1.at[m, q, part], r1[m].at[q, part], phase1[q]) for q in range(4)])
-        copies2.append([remote(s2.at[m, d, part], r2[m].at[zf, d, part], dev) for zf, d, dev in phase2])
-        rims.append([
-            remote(rim_out.at[m, 0], rim_in.at[m, 0], {"comp": c, "gx": (g + 1) % 8, "gy": y}),
-            remote(rim_out.at[m, 1], rim_in.at[m, 1], {"comp": c, "gx": (g + 7) % 8, "gy": y}),
-            remote(rim_out.at[m, 2], rim_in.at[m, 2], north),
-            remote(rim_out.at[m, 3], rim_in.at[m, 3], south),
-        ])
+    swap_face = remote(face_out, face_in, mates[0][2])
+    copies1 = [remote(s1.at[q], r1.at[q], phase1[q]) for q in range(4)]
+    copies2 = [remote(s2.at[d], r2.at[zf, d], dev) for zf, d, dev in phase2]
+    uas = [remote(ua_out.at[d], ua_in.at[zf, d], dev) for zf, d, dev in mates]
+    ubs = [remote(ub_out.at[d], ub_in.at[d], place(c, z, x + d)) for d in range(1, 4)]
+    patches = [remote(patch_out, patch_in.at[zf, d], dev) for zf, d, dev in mates]
+    around = [
+        {"comp": c, "gx": (g + 1) % 8, "gy": y},
+        {"comp": c, "gx": (g + 7) % 8, "gy": y},
+        north,
+        south,
+    ]
+    rims = [
+        [remote(rim_out.at[m, k, part], rim_in.at[m, k, part], around[k])
+         for k, part in enumerate([pl.ds(0, 48)] * 2 + [pl.ds(0, 40)] * 2)]
+        for m in range(2)
+    ]
+    edges = [remote(edge_out.at[k], edge_in.at[k], around[k]) for k in range(4)]
+    sides = []
+    base = count[0]
+    for k in range(2):
+        for zz in range(2):
+            n = 2 * k + zz
+            sides.append(pltpu.make_async_remote_copy(
+                src_ref=side_out.at[k], dst_ref=side_in.at[g], send_sem=send_sem.at[base + n],
+                recv_sem=side_sem.at[g], device_id=place(other, zz, 3 * k), device_id_type=MESH,
+            ))
+    sides_in = [
+        pltpu.make_async_remote_copy(
+            src_ref=side_out.at[0], dst_ref=side_in.at[i], send_sem=send_sem.at[base],
+            recv_sem=side_sem.at[i], device_id=mates[0][2], device_id_type=MESH,
+        )
+        for i in range(8)
+    ]
+    has = [x < 3, x > 0, y < last_y, y > 0]
+    gets = [x > 0, x < 3, y > 0, y < last_y]
 
     def start_rims(m):
         rims[m][0].start()
         rims[m][1].start()
-
-        @pl.when(y < last_y)
-        def _():
-            rims[m][2].start()
-
-        @pl.when(y > 0)
-        def _():
-            rims[m][3].start()
+        for k in (2, 3):
+            pl.when(has[k])(rims[m][k].start)
 
     def wait_rims(m):
         rims[m][0].wait_recv()
         rims[m][1].wait_recv()
-
-        @pl.when(y > 0)
-        def _():
-            rims[m][2].wait_recv()
-
-        @pl.when(y == 0)
-        def _():
-            rim_in[m, 2] = jnp.zeros((FACE, 128), F32)
-
-        @pl.when(y < last_y)
-        def _():
-            rims[m][3].wait_recv()
-
-        @pl.when(y == last_y)
-        def _():
-            rim_in[m, 3] = jnp.zeros((FACE, 128), F32)
-
-    def forward(m):
-        for copy in copies1[m]:
+        for k in (2, 3):
+            pl.when(gets[k])(rims[m][k].wait_recv)
+
+            @pl.when(jnp.logical_not(gets[k]))
+            def _():
+                rim_in[m, k] = jnp.zeros((48, 128), F32)
+
+    def forward():
+        for copy in copies1:
             copy.wait_recv()
         for d in range(4):
-            s2[m, d, 0 : piece[m]] = r1[m][(8 - d - shift) % 4, 0 : piece[m]]
-        for copy in copies2[m]:
+            s2[d] = r1[(8 - d - shift) % 4]
+        for copy in copies2:
             copy.start()
-        r2[m][0, 0, 0 : piece[m]] = s2[m, 0, 0 : piece[m]]
-
-    def collect(m):
-        for copy in copies2[m]:
-            copy.wait_recv()
-        q = [r2[m][z_pick, (8 - i - shift) % 4, 0 : piece[m]] for i in range(4)]
+        r2[0, 0] = s2[0]
+
+    def joined(q):
         left = jnp.concatenate([q[0][0:40], q[1][0:40]], axis=0)
         right = jnp.concatenate([q[2][0:40], q[3][0:40]], axis=0)
-        wet = None if m == 0 else jnp.concatenate([q[0][40:41], q[2][40:41]], axis=1)
-        return jnp.concatenate([left, right], axis=1), wet
-
-    start_rims(0)
-    for copy in copies1[0]:
-        copy.start()
-    swap_face.start()
+        return jnp.concatenate([left, right], axis=1)
+
+    def collect():
+        for copy in copies2:
+            copy.wait_recv()
+        return joined([r2[z_pick, (8 - i - shift) % 4] for i in range(4)])
+
+    def forward_base():
+        for copy in uas:
+            copy.wait_recv()
+        for d in range(4):
+            z_of = (z * 4 + (x + d) % 4 + delta) % 8 // 4
+            ub_out[d] = ua_in[jnp.where(z_of == z, 0, 1), (8 - d - shift) % 4]
+        for copy in ubs:
+            copy.start()
+        ub_in[0] = ub_out[0]
 
     wide = iota((FACE, COLS), 1)
 
@@ -301,106 +360,219 @@
         term = (term.reshape(5, 64, COLS) * weight[None]).reshape(ROWS, COLS)
         return (term + lifted) * mask
 
-    def rim_part(m, layer):
-        packed = [rim_in[m, k] for k in range(4)]
-        west = jnp.where(lane < 16, pltpu.roll(packed[0], (128 - 16 * layer) % 128, 1), 0.0)
-        east = jnp.where(lane >= 112, pltpu.roll(packed[1], 112 - 16 * layer, 1), 0.0)
+    def rim_lift(west, east, near, far):
         none = jnp.zeros((FACE, 128), F32)
-        near, far = [], []
-        for half in range(2):
-            step = layer + 4 * half
-            near.append(jnp.where(lane % 16 == 0, pltpu.roll(packed[2], (128 - step) % 128, 1), 0.0))
-            far.append(jnp.where(lane % 16 == 15, pltpu.roll(packed[3], (143 - step) % 128, 1), 0.0))
-        j3[0:SLOT] = split3(jnp.concatenate([west, none], axis=1))
-        j3[SLOT : 2 * SLOT] = split3(jnp.concatenate([none, east], axis=1))
+        j3[0:SLOT] = split3(jnp.concatenate([jnp.where(lane < 16, west, 0.0), none], axis=1))
+        j3[SLOT : 2 * SLOT] = split3(jnp.concatenate([none, jnp.where(lane >= 112, east, 0.0)], axis=1))
+        near = [jnp.where(lane % 16 == 0, v, 0.0) for v in near]
+        far = [jnp.where(lane % 16 == 15, v, 0.0) for v in far]
         j3[2 * SLOT : 3 * SLOT] = split3(jnp.concatenate(near, axis=1))
         j3[3 * SLOT : 4 * SLOT] = split3(jnp.concatenate(far, axis=1))
         return jnp.dot(
             lift[:, 0 : 4 * SLOT], j3[0 : 4 * SLOT], preferred_element_type=F32
         ) * mask
 
+    def unfold_rims(m):
+        for k in range(4):
+            rim_full[k] = unfold_half(rim_in[m, k, 0:40], 64 if k < 2 else 8)
+
+    def rim_part(layer):
+        return rim_lift(
+            pltpu.roll(rim_full[0], (128 - 16 * layer) % 128, 1),
+            pltpu.roll(rim_full[1], 112 - 16 * layer, 1),
+            [pltpu.roll(rim_full[2], (128 - layer - 4 * h) % 128, 1) for h in range(2)],
+            [pltpu.roll(rim_full[3], (143 - layer - 4 * h) % 128, 1) for h in range(2)],
+        )
+
     def interface_part(block):
         op = lift[:, pl.ds(pl.multiple_of((4 + c) * SLOT, SLOT), SLOT)]
         return jnp.dot(op, split3(block), preferred_element_type=F32) * mask
 
-    def first(layer, carry):
+    def first(layer):
         put(w, layer, get(start, layer) + local(start, layer))
+
+    first(surface)
+    held = surface_trace(w)
+    pack_block(held, ua_out)
+    for q in range(4):
+        ua_out[q, 40:48] = jnp.broadcast_to(mask[:, 128 * (q // 2) : 128 * (q // 2) + 128], (8, 128))
+
+    pl.semaphore_wait(
+        barrier, 15 + jnp.where(y < last_y, 1, 0) + jnp.where(y > 0, 1, 0)
+    )
+
+    start_rims(0)
+    for copy in copies1 + uas + sides + [swap_face]:
+        copy.start()
+
+    def others(step):
+        def run(i, carry):
+            step(i + 1 - c)
+            return carry
+
+        lax.fori_loop(0, LEV - 1, run, 0)
+
+    others(first)
+    forward()
+
+    wait_rims(0)
+    unfold_rims(0)
+    here = (128 - 3 * c) % 128
+    level = [
+        pltpu.roll(rim_full[0], (128 - 48 * c) % 128, 1),
+        pltpu.roll(rim_full[1], (128 - 48 * c) % 128, 1),
+    ] + [
+        jnp.where(lane % 16 == 0, pltpu.roll(rim_full[k], here, 1), pltpu.roll(rim_full[k], (125 - 3 * c) % 128, 1))
+        for k in (2, 3)
+    ]
+    for k in range(4):
+        patch_rows[FACE * k : FACE * k + FACE] = jnp.dot(
+            small[k], split3(level[k]), preferred_element_type=F32
+        )
+    nodes = jnp.where(
+        c == 0, patch_rows[pl.ds(0, FACE, stride=4), :], patch_rows[pl.ds(3, FACE, stride=4), :]
+    )
+    lane8 = iota((8, 128), 1)
+    folded = [jnp.zeros((8, 128), F32)] * 2
+    for r in range(5):
+        tile = nodes[8 * r : 8 * r + 8]
+        folded[0] = jnp.where(lane8 // 16 == r, pltpu.roll(tile, 16 * r, 1), folded[0])
+        tile = nodes[40 + 8 * r : 48 + 8 * r]
+        folded[1] = jnp.where(lane8 % 16 // 2 == r, pltpu.roll(tile, 2 * r, 1), folded[1])
+    patch_out[...] = jnp.concatenate(folded, axis=0)
+    for copy in patches:
+        copy.start()
+
+    def first_rims(layer, carry):
+        put(w, layer, get(w, layer) + rim_part(layer))
         return carry
 
-    lax.fori_loop(0, LEV, first, 0)
-    forward(0)
-    wait_rims(0)
-
-    def first_rims(layer, carry):
-        put(w, layer, get(w, layer) + rim_part(0, layer))
-        return carry
-
     lax.fori_loop(0, LEV, first_rims, 0)
-
-    held = surface_trace(w)
-    pack_block(held, s1.at[1])
-    for q in range(4):
-        s1[1, q, 40:48] = jnp.broadcast_to(mask[:, 128 * (q // 2) : 128 * (q // 2) + 128], (8, 128))
-    for copy in copies1[1]:
-        copy.start()
-    swap_face.wait_recv()
-    own = surface_trace(start)
-    reply = jnp.dot(face_in[...].astype(BF16), split3(own), preferred_element_type=F32)
-    forward(1)
-
-    block, _ = collect(0)
-    put(w, surface, get(w, surface) + interface_part(block))
-
     pack_rims(w, rim_out.at[1])
     start_rims(1)
 
-    def second(layer, carry):
-        put(acc, layer, get(start, layer) + get(w, layer) + local(w, layer))
-        return carry
-
-    lax.fori_loop(0, LEV, second, 0)
+    swap_face.wait_recv()
+    reply = jnp.dot(face_in[...].astype(BF16), split3(surface_trace(start)), preferred_element_type=F32)
+
+    def second(layer):
+        acc[:, layer_lanes(layer)] = get(start, layer) + get(w, layer) + local(w, layer)
+
+    others(second)
+    forward_base()
+
+    put(w, surface, get(w, surface) + interface_part(collect()))
+
+    v0, v1 = w[2 * surface], w[2 * surface + 1]
+    first_two = lane % 16 == 0
+    edge_out[0] = fold_x(pltpu.roll(a_trace(v1, 1), 16, 1))
+    edge_out[1] = fold_x(a_trace(v0, 0))
+    edge_out[2] = fold_y(
+        jnp.where(first_two, pltpu.roll(b_trace(v0, 1), 113, 1), pltpu.roll(b_trace(v1, 1), 114, 1))
+    )
+    edge_out[3] = fold_y(jnp.where(first_two, b_trace(v0, 0), pltpu.roll(b_trace(v1, 0), 1, 1)))
+    for k in range(4):
+        pl.when(has[k])(edges[k].start)
+
+    second(surface)
     wait_rims(1)
-
-    def second_rims(layer, carry):
-        put(acc, layer, 0.5 * (get(acc, layer) + rim_part(1, layer)))
-        return carry
-
-    lax.fori_loop(0, LEV, second_rims, 0)
-    block, wet = collect(1)
-    put(acc, surface, get(acc, surface) + 0.5 * interface_part(block + wet * reply))
-
-    stores = [
-        pltpu.make_async_copy(acc.at[t], out_hbm.at[:, 128 * t : 128 * t + 128], local_sem.at[13 + t])
-        for t in range(8)
-    ]
-    for store in stores:
-        store.start()
-    for copies in [[swap_face]] + copies1 + copies2:
-        for copy in copies:
-            copy.wait_send()
+    unfold_rims(1)
+
+    def second_rims(layer):
+        lanes = layer_lanes(layer)
+        acc[:, lanes] = 0.5 * (acc[:, lanes] + rim_part(layer))
+
+    others(second_rims)
+
+    def finish_edge(k):
+        for copy in sides_in:
+            copy.wait_recv()
+        partner = (g + (7 if k == 0 else 1) + delta) % 8
+        row = iota((FACE, FACE), 0)
+        col = iota((FACE, FACE), 1)
+        pick = (
+            (row // 16 == col // 16) & (row % 4 == 3 * c) & (col % 4 == row // 4 % 4)
+            & (col // 4 % 4 == (3 if k == 0 else 0))
+        ).astype(BF16)
+        op = jnp.dot(pick, small[4 + c], preferred_element_type=F32).astype(BF16)
+        term = jnp.dot(op, split3(unfold_x(side_in[partner])), preferred_element_type=F32)
+        held = pltpu.roll(rim_full[k], (128 - 48 * c) % 128, 1)
+        rim_edge[k] = held + term * rim_in[0, k, 40:41]
+
+    def take_edge(k):
+        edges[k].wait_recv()
+        rim_edge[k] = unfold_x(edge_in[k]) if k < 2 else unfold_y(edge_in[k])
+
+    for k in range(4):
+        pl.when(gets[k])(functools.partial(take_edge, k))
+
+        @pl.when(jnp.logical_not(gets[k]))
+        def _():
+            if k < 2:
+                finish_edge(k)
+            else:
+                rim_edge[k] = jnp.zeros((FACE, 128), F32)
+
+    part = rim_lift(
+        rim_edge[0],
+        pltpu.roll(rim_edge[1], 112, 1),
+        [rim_edge[2], pltpu.roll(rim_edge[2], 127, 1)],
+        [pltpu.roll(rim_edge[3], 15, 1), pltpu.roll(rim_edge[3], 14, 1)],
+    )
+    lanes = layer_lanes(surface)
+    acc[:, lanes] = 0.5 * (acc[:, lanes] + part)
+
+    for copy in ubs + patches:
+        copy.wait_recv()
+    q = [ub_in[(8 - i - shift) % 4] for i in range(4)]
+    wet = jnp.concatenate([q[0][40:41], q[2][40:41]], axis=1)
+    patch = patch_in[z_pick, (4 - shift) % 4]
+    tiles = [pltpu.roll(patch[0:8], (128 - 16 * r) % 128, 1) for r in range(5)]
+    tiles += [pltpu.roll(patch[8:16], (128 - 2 * r) % 128, 1) for r in range(5)]
+    packed = jnp.concatenate(tiles, axis=0)
+    high = packed.astype(BF16)
+    low = (packed - high.astype(F32)).astype(BF16)
+    row = iota((2 * FACE, FACE), 0)
+    col = iota((2 * FACE, FACE), 1)
+    node, face, index = row % FACE, col // 20, col % 20
+    target = index // 4 * 16 + jnp.where(face < 2, index % 4 + 12 * face, index % 4 * 4 + 3 * (face - 2))
+    to_node = ((node == target) & (row // FACE == face // 2)).astype(BF16)
+    spread = jnp.dot(to_node, high, preferred_element_type=F32) + jnp.dot(
+        to_node, low, preferred_element_type=F32
+    )
+    on_x, on_y = spread[0:FACE], spread[FACE:]
+    node = iota((FACE, 128), 0)
+    node_a, node_b = node // 4 % 4, node % 4
+    halves = []
+    for h in range(2):
+        side = (
+            jnp.where((lane < 16) & (node_a == 0), on_x, 0.0)
+            if h == 0
+            else jnp.where((lane >= 112) & (node_a == 3), pltpu.roll(on_x, 112, 1), 0.0)
+        )
+        near = jnp.where((lane % 16 == 0) & (node_b == 0), pltpu.roll(on_y, (128 - h) % 128, 1), 0.0)
+        far = jnp.where((lane % 16 == 15) & (node_b == 3), pltpu.roll(on_y, 15 - h, 1), 0.0)
+        halves.append(side + near + far)
+    block = joined(q) + wet * (jnp.concatenate(halves, axis=1) + reply)
+    acc[:, lanes] = acc[:, lanes] + 0.5 * interface_part(block)
+
+    for copy in [swap_face] + copies1 + copies2 + uas + ubs + patches + sides:
+        copy.wait_send()
     for m in range(2):
         rims[m][0].wait_send()
         rims[m][1].wait_send()
-
-        @pl.when(y < last_y)
-        def _():
-            rims[m][2].wait_send()
-
-        @pl.when(y > 0)
-        def _():
-            rims[m][3].wait_send()
-
-    for store in stores:
-        store.wait()
+        for k in (2, 3):
+            pl.when(has[k])(rims[m][k].wait_send)
+    for k in range(4):
+        pl.when(has[k])(edges[k].wait_send)
 
 
 def body(cotangent, metric, volume_ops, face_ops, land_mask, intersection):
-    copies = 31
+    copies = 47
     out = pl.pallas_call(
         kernel,
         out_shape=jax.ShapeDtypeStruct((ROWS, LEV * COLS), F32),
-        in_specs=[pl.BlockSpec(memory_space=pl.ANY)] * 6,
-        out_specs=pl.BlockSpec(memory_space=pl.ANY),
+        in_specs=[pl.BlockSpec(memory_space=pltpu.HBM)] * 6,
+        out_specs=pl.BlockSpec(memory_space=pltpu.VMEM),
         scratch_shapes=[
             pltpu.SMEM((16,), jnp.int32),
             pltpu.VMEM((2 * LEV, ROWS, 128), F32),
@@ -409,34 +581,50 @@
             pltpu.VMEM((6, FACE, FACE), F32),
             pltpu.VMEM((1, COLS), jnp.int32),
             pltpu.VMEM((2 * LEV, ROWS, 128), F32),
-            pltpu.VMEM((2 * LEV, ROWS, 128), F32),
             pltpu.VMEM((ROWS, 6 * SLOT), BF16),
             pltpu.VMEM((6, FACE, SLOT), BF16),
             pltpu.VMEM((6 * SLOT, COLS), BF16),
             pltpu.VMEM((FACE, SLOT), F32),
             pltpu.VMEM((FACE, SLOT), F32),
-            pltpu.VMEM((2, 4, FACE, 128), F32),
-            pltpu.VMEM((2, 4, FACE, 128), F32),
+            pltpu.VMEM((2, 4, 48, 128), F32),
             pltpu.VMEM((2, 4, 48, 128), F32),
             pltpu.VMEM((4, 40, 128), F32),
+            pltpu.VMEM((4, 40, 128), F32),
+            pltpu.VMEM((4, 40, 128), F32),
+            pltpu.VMEM((2, 4, 40, 128), F32),
             pltpu.VMEM((4, 48, 128), F32),
             pltpu.VMEM((2, 4, 48, 128), F32),
-            pltpu.VMEM((2, 4, 40, 128), F32),
-            pltpu.VMEM((2, 4, 48, 128), F32),
-            pltpu.SemaphoreType.DMA((21,)),
+            pltpu.VMEM((4, 48, 128), F32),
+            pltpu.VMEM((4, 48, 128), F32),
+            pltpu.VMEM((ROWS, 128), F32),
+            pltpu.VMEM((16, 128), F32),
+            pltpu.VMEM((2, 4, 16, 128), F32),
+            pltpu.VMEM((2, 16, 128), F32),
+            pltpu.VMEM((8, 16, 128), F32),
+            pltpu.VMEM((4, 16, 128), F32),
+            pltpu.VMEM((4, 16, 128), F32),
+            pltpu.VMEM((4, FACE, 128), F32),
+            pltpu.VMEM((4, FACE, 128), F32),
+            pltpu.SemaphoreType.DMA((13,)),
             pltpu.SemaphoreType.DMA((copies,)),
             pltpu.SemaphoreType.DMA((copies,)),
+            pltpu.SemaphoreType.DMA((8,)),
         ],
         compiler_params=pltpu.CompilerParams(
             collective_id=0, has_side_effects=True, vmem_limit_bytes=48 * 1024 * 1024
         ),
     )(
-        intersection,
-        cotangent[0, 0, 0],
-        metric[0, 0, 0],
-        volume_ops[0],
-        face_ops[0],
-        land_mask[0],
+        *(
+            pltpu.with_memory_space_constraint(a, pltpu.HBM)
+            for a in (
+                intersection,
+                cotangent[0, 0, 0],
+                metric[0, 0, 0],
+                volume_ops[0],
+                face_ops[0],
+                land_mask[0],
+            )
+        )
     )
     return out[None, None, None]
 

time: 39.8 us -> 31.3 us (0.79)
  the two profiles are of different devices: /device:TPU:25 before, /device:TPU:33 now
where the time goes in v2:
time: 31.3 us; the launch traced here: 31 us
  Pallas kernels  29.9 us (96%)
  local copies, waits for them, and re-layouts  1.06 us (3%)
    pallas_call x1, Pallas kernels, body(): pl.pallas_call(kernel, out_shape=jax.ShapeDtypeStruct((ROWS, LEV * COLS),...  29.9 us
    unnamed x1, local copies, waits for them, and re-layouts  1.06 us

profile of v2, /device:TPU:33, one launch (start us, length us, event | category | flops | bytes accessed | tf_op | source)
XLA Modules:
  0.0 31.0 jit_solution(4163208937311278132)
XLA Ops:
  0.0 29.9 %shard_map.64 = f32[320,1024]{1,0:T(8,128)S(1)} custom-call(s32[16]{0:T(128)} %inter_hbm.1, f32[320,1024]{1,0:T(8,128)} %bitcast.7, f32[64,1024]{1,0:T(8,128)} %bitcast.8, bf16[320,320]{1,0:T(8,128)(2,1)} %bitcast.9, f32[6,80,80]{2,1,0:T(8,128)} %bitcast.10, s32[1,256]{1,0:T(1,128)} %bitcast.11), custom_call_target="tpu_custom_call" | custom-call | tf_op jit(solution)/shard_map/pallas_call | solution.py:571
  30.0 1.1 %copy.8 = f32[1,1,1,320,1024]{4,3,2,1,0:T(8,128)} copy(f32[1,1,1,320,1024]{4,3,2,1,0:T(8,128)S(1)} %bitcast.6) | data formatting | bytes 2621440

commit v3 on v2

--- a/solution.py
+++ b/solution.py
@@ -124,7 +124,7 @@
     inter, start, metric, volume, faces, mask_i,
     w, lift, small, j3, face_out, face_in,
     rim_out, rim_in, s1, r1, s2, r2, ua_out, ua_in, ub_out, ub_in,
-    patch_rows, patch_out, patch_in, side_out, side_in, edge_out, edge_in, rim_edge, rim_full,
+    patch_rows, patch_out, patch_in, side_out, side_in, edge_out, edge_in, rim_edge, terms,
     local_sem, send_sem, recv_sem, side_sem,
 ):
     c = lax.axis_index("comp")
@@ -226,26 +226,6 @@
     side_out[0] = fold_x(pltpu.roll(own[:, 128:256], 16, 1))
     side_out[1] = fold_x(own[:, 0:128])
 
-    loads[9].wait()
-    row = iota((FACE, SLOT), 0)
-    col = iota((FACE, SLOT), 1)
-    to_high = ((col == row) | (col == row + FACE)).astype(BF16)
-    to_low = (col == row + 2 * FACE).astype(BF16)
-    for face in range(6):
-        scaled = STEP * faces[face]
-        high = scaled.astype(BF16)
-        low = (scaled - high.astype(F32)).astype(BF16)
-        spread = jnp.dot(high, to_high, preferred_element_type=F32) + jnp.dot(
-            low, to_low, preferred_element_type=F32
-        )
-        small[face] = spread.astype(BF16)
-        lift[:, face * SLOT : face * SLOT + SLOT] = jnp.dot(
-            placement(face), small[face], preferred_element_type=F32
-        ).astype(BF16)
-    face_out[...] = small[4 + c].astype(F32)
-
-    loads[10].wait()
-    loads[11].wait()
     loads[12].wait()
 
     off = inter[y]
@@ -360,29 +340,42 @@
         term = (term.reshape(5, 64, COLS) * weight[None]).reshape(ROWS, COLS)
         return (term + lifted) * mask
 
-    def rim_lift(west, east, near, far):
-        none = jnp.zeros((FACE, 128), F32)
-        j3[0:SLOT] = split3(jnp.concatenate([jnp.where(lane < 16, west, 0.0), none], axis=1))
-        j3[SLOT : 2 * SLOT] = split3(jnp.concatenate([none, jnp.where(lane >= 112, east, 0.0)], axis=1))
-        near = [jnp.where(lane % 16 == 0, v, 0.0) for v in near]
-        far = [jnp.where(lane % 16 == 15, v, 0.0) for v in far]
-        j3[2 * SLOT : 3 * SLOT] = split3(jnp.concatenate(near, axis=1))
-        j3[3 * SLOT : 4 * SLOT] = split3(jnp.concatenate(far, axis=1))
-        return jnp.dot(
-            lift[:, 0 : 4 * SLOT], j3[0 : 4 * SLOT], preferred_element_type=F32
-        ) * mask
+    def lift_rims(rims):
+        upper = iota((FACE, 128), 0) % 8 >= 4
+        for k in range(4):
+            r = jnp.dot(small[k], split3(rims[k]), preferred_element_type=F32)
+            terms[k] = r
+            if k == 2:
+                terms[4] = jnp.where(upper, 0.0, r)
+                terms[5] = jnp.where(upper, 0.0, pltpu.roll(r, FACE - 4, 0))
+            if k == 3:
+                terms[6] = jnp.where(upper, pltpu.roll(r, 4, 0), 0.0)
+                terms[7] = jnp.where(upper, r, 0.0)
+
+    def spread_rims(half, to_x, to_near, to_far):
+        if half == 0:
+            side = jnp.where(lane < 16, pltpu.roll(terms[0], to_x, 1), 0.0)
+        else:
+            side = jnp.where(lane >= 112, pltpu.roll(terms[1], to_x, 1), 0.0)
+        near = [jnp.where(lane % 16 == 0, pltpu.roll(terms[4 + i], to_near, 1), 0.0) for i in range(2)]
+        far = [jnp.where(lane % 16 == 15, pltpu.roll(terms[6 + i], to_far, 1), 0.0) for i in range(2)]
+        tiles = []
+        for r in range(10):
+            for i in range(2):
+                for k in range(2):
+                    tile = (far if k else near)[i][8 * r : 8 * r + 8]
+                    if r % 2 == half and i == half:
+                        tile = tile + side[r // 2 * 16 + 8 * k : r // 2 * 16 + 8 * k + 8]
+                    tiles.append(tile)
+        return jnp.concatenate(tiles, axis=0) * mask[:, 128 * half : 128 * half + 128]
+
+    def layer_rims(half, layer):
+        step = layer + 4 * half
+        to_x = (128 - 16 * layer) % 128 if half == 0 else 112 - 16 * layer
+        return spread_rims(half, to_x, (128 - step) % 128, (143 - step) % 128)
 
     def unfold_rims(m):
-        for k in range(4):
-            rim_full[k] = unfold_half(rim_in[m, k, 0:40], 64 if k < 2 else 8)
-
-    def rim_part(layer):
-        return rim_lift(
-            pltpu.roll(rim_full[0], (128 - 16 * layer) % 128, 1),
-            pltpu.roll(rim_full[1], 112 - 16 * layer, 1),
-            [pltpu.roll(rim_full[2], (128 - layer - 4 * h) % 128, 1) for h in range(2)],
-            [pltpu.roll(rim_full[3], (143 - layer - 4 * h) % 128, 1) for h in range(2)],
-        )
+        return [unfold_half(rim_in[m, k, 0:40], 64 if k < 2 else 8) for k in range(4)]
 
     def interface_part(block):
         op = lift[:, pl.ds(pl.multiple_of((4 + c) * SLOT, SLOT), SLOT)]
@@ -391,18 +384,43 @@
     def first(layer):
         put(w, layer, get(start, layer) + local(start, layer))
 
-    first(surface)
-    held = surface_trace(w)
-    pack_block(held, ua_out)
-    for q in range(4):
-        ua_out[q, 40:48] = jnp.broadcast_to(mask[:, 128 * (q // 2) : 128 * (q // 2) + 128], (8, 128))
+    def prepare():
+        for load in loads[9:12]:
+            load.wait()
+        row = iota((FACE, SLOT), 0)
+        col = iota((FACE, SLOT), 1)
+        to_high = ((col == row) | (col == row + FACE)).astype(BF16)
+        to_low = (col == row + 2 * FACE).astype(BF16)
+        for face in range(6):
+            scaled = STEP * faces[face]
+            high = scaled.astype(BF16)
+            low = (scaled - high.astype(F32)).astype(BF16)
+            spread = jnp.dot(high, to_high, preferred_element_type=F32) + jnp.dot(
+                low, to_low, preferred_element_type=F32
+            )
+            small[face] = spread.astype(BF16)
+            lift[:, face * SLOT : face * SLOT + SLOT] = jnp.dot(
+                placement(face), small[face], preferred_element_type=F32
+            ).astype(BF16)
+        face_out[...] = small[4 + c].astype(F32)
+
+        first(surface)
+        held = surface_trace(w)
+        pack_block(held, ua_out)
+        for q in range(4):
+            ua_out[q, 40:48] = jnp.broadcast_to(mask[:, 128 * (q // 2) : 128 * (q // 2) + 128], (8, 128))
 
     pl.semaphore_wait(
         barrier, 15 + jnp.where(y < last_y, 1, 0) + jnp.where(y > 0, 1, 0)
     )
 
     start_rims(0)
-    for copy in copies1 + uas + sides + [swap_face]:
+    for copy in copies1 + sides:
+        copy.start()
+
+    prepare()
+
+    for copy in uas + [swap_face]:
         copy.start()
 
     def others(step):
@@ -416,40 +434,37 @@
     forward()
 
     wait_rims(0)
-    unfold_rims(0)
-    here = (128 - 3 * c) % 128
-    level = [
-        pltpu.roll(rim_full[0], (128 - 48 * c) % 128, 1),
-        pltpu.roll(rim_full[1], (128 - 48 * c) % 128, 1),
-    ] + [
-        jnp.where(lane % 16 == 0, pltpu.roll(rim_full[k], here, 1), pltpu.roll(rim_full[k], (125 - 3 * c) % 128, 1))
-        for k in (2, 3)
-    ]
+    lift_rims(unfold_rims(0))
+    def first_rims(layer, carry):
+        for half in range(2):
+            w[2 * layer + half] = w[2 * layer + half] + layer_rims(half, layer)
+        return carry
+
+    lax.fori_loop(0, LEV, first_rims, 0)
+    pack_rims(w, rim_out.at[1])
+    start_rims(1)
+
     for k in range(4):
-        patch_rows[FACE * k : FACE * k + FACE] = jnp.dot(
-            small[k], split3(level[k]), preferred_element_type=F32
-        )
+        patch_rows[FACE * k : FACE * k + FACE] = terms[k]
     nodes = jnp.where(
         c == 0, patch_rows[pl.ds(0, FACE, stride=4), :], patch_rows[pl.ds(3, FACE, stride=4), :]
+    )
+    on_x = pltpu.roll(nodes[0:40], (128 - 48 * c) % 128, 1)
+    on_y = jnp.where(
+        iota((40, 128), 1) % 16 == 0,
+        pltpu.roll(nodes[40:80], (128 - 3 * c) % 128, 1),
+        pltpu.roll(nodes[40:80], 125 - 3 * c, 1),
     )
     lane8 = iota((8, 128), 1)
     folded = [jnp.zeros((8, 128), F32)] * 2
     for r in range(5):
-        tile = nodes[8 * r : 8 * r + 8]
+        tile = on_x[8 * r : 8 * r + 8]
         folded[0] = jnp.where(lane8 // 16 == r, pltpu.roll(tile, 16 * r, 1), folded[0])
-        tile = nodes[40 + 8 * r : 48 + 8 * r]
+        tile = on_y[8 * r : 8 * r + 8]
         folded[1] = jnp.where(lane8 % 16 // 2 == r, pltpu.roll(tile, 2 * r, 1), folded[1])
     patch_out[...] = jnp.concatenate(folded, axis=0)
     for copy in patches:
         copy.start()
-
-    def first_rims(layer, carry):
-        put(w, layer, get(w, layer) + rim_part(layer))
-        return carry
-
-    lax.fori_loop(0, LEV, first_rims, 0)
-    pack_rims(w, rim_out.at[1])
-    start_rims(1)
 
     swap_face.wait_recv()
     reply = jnp.dot(face_in[...].astype(BF16), split3(surface_trace(start)), preferred_element_type=F32)
@@ -475,51 +490,14 @@
 
     second(surface)
     wait_rims(1)
-    unfold_rims(1)
+    lift_rims(unfold_rims(1))
 
     def second_rims(layer):
+        part = jnp.concatenate([layer_rims(0, layer), layer_rims(1, layer)], axis=1)
         lanes = layer_lanes(layer)
-        acc[:, lanes] = 0.5 * (acc[:, lanes] + rim_part(layer))
+        acc[:, lanes] = 0.5 * (acc[:, lanes] + part)
 
     others(second_rims)
-
-    def finish_edge(k):
-        for copy in sides_in:
-            copy.wait_recv()
-        partner = (g + (7 if k == 0 else 1) + delta) % 8
-        row = iota((FACE, FACE), 0)
-        col = iota((FACE, FACE), 1)
-        pick = (
-            (row // 16 == col // 16) & (row % 4 == 3 * c) & (col % 4 == row // 4 % 4)
-            & (col // 4 % 4 == (3 if k == 0 else 0))
-        ).astype(BF16)
-        op = jnp.dot(pick, small[4 + c], preferred_element_type=F32).astype(BF16)
-        term = jnp.dot(op, split3(unfold_x(side_in[partner])), preferred_element_type=F32)
-        held = pltpu.roll(rim_full[k], (128 - 48 * c) % 128, 1)
-        rim_edge[k] = held + term * rim_in[0, k, 40:41]
-
-    def take_edge(k):
-        edges[k].wait_recv()
-        rim_edge[k] = unfold_x(edge_in[k]) if k < 2 else unfold_y(edge_in[k])
-
-    for k in range(4):
-        pl.when(gets[k])(functools.partial(take_edge, k))
-
-        @pl.when(jnp.logical_not(gets[k]))
-        def _():
-            if k < 2:
-                finish_edge(k)
-            else:
-                rim_edge[k] = jnp.zeros((FACE, 128), F32)
-
-    part = rim_lift(
-        rim_edge[0],
-        pltpu.roll(rim_edge[1], 112, 1),
-        [rim_edge[2], pltpu.roll(rim_edge[2], 127, 1)],
-        [pltpu.roll(rim_edge[3], 15, 1), pltpu.roll(rim_edge[3], 14, 1)],
-    )
-    lanes = layer_lanes(surface)
-    acc[:, lanes] = 0.5 * (acc[:, lanes] + part)
 
     for copy in ubs + patches:
         copy.wait_recv()
@@ -553,7 +531,43 @@
         far = jnp.where((lane % 16 == 15) & (node_b == 3), pltpu.roll(on_y, 15 - h, 1), 0.0)
         halves.append(side + near + far)
     block = joined(q) + wet * (jnp.concatenate(halves, axis=1) + reply)
-    acc[:, lanes] = acc[:, lanes] + 0.5 * interface_part(block)
+    lanes = layer_lanes(surface)
+    acc[:, lanes] = 0.5 * (acc[:, lanes] + interface_part(block))
+
+    def finish_edge(k):
+        for copy in sides_in:
+            copy.wait_recv()
+        partner = (g + (7 if k == 0 else 1) + delta) % 8
+        row = iota((FACE, FACE), 0)
+        col = iota((FACE, FACE), 1)
+        pick = (
+            (row // 16 == col // 16) & (row % 4 == 3 * c) & (col % 4 == row // 4 % 4)
+            & (col // 4 % 4 == (3 if k == 0 else 0))
+        ).astype(BF16)
+        op = jnp.dot(pick, small[4 + c], preferred_element_type=F32).astype(BF16)
+        term = jnp.dot(op, split3(unfold_x(side_in[partner])), preferred_element_type=F32)
+        held = pltpu.roll(unfold_half(rim_in[1, k, 0:40], 64), (128 - 48 * c) % 128, 1)
+        rim_edge[k] = held + term * rim_in[0, k, 40:41]
+
+    def take_edge(k):
+        edges[k].wait_recv()
+        rim_edge[k] = unfold_x(edge_in[k]) if k < 2 else unfold_y(edge_in[k])
+
+    for k in range(4):
+        pl.when(gets[k])(functools.partial(take_edge, k))
+
+        @pl.when(jnp.logical_not(gets[k]))
+        def _():
+            if k < 2:
+                finish_edge(k)
+            else:
+                rim_edge[k] = jnp.zeros((FACE, 128), F32)
+
+    lift_rims([rim_edge[k] for k in range(4)])
+    part = jnp.concatenate(
+        [spread_rims(0, 0, 0, 15), spread_rims(1, 112, 127, 14)], axis=1
+    )
+    acc[:, lanes] = acc[:, lanes] + 0.5 * part
 
     for copy in [swap_face] + copies1 + copies2 + uas + ubs + patches + sides:
         copy.wait_send()
@@ -604,7 +618,7 @@
             pltpu.VMEM((4, 16, 128), F32),
             pltpu.VMEM((4, 16, 128), F32),
             pltpu.VMEM((4, FACE, 128), F32),
-            pltpu.VMEM((4, FACE, 128), F32),
+            pltpu.VMEM((8, FACE, 128), F32),
             pltpu.SemaphoreType.DMA((13,)),
             pltpu.SemaphoreType.DMA((copies,)),
             pltpu.SemaphoreType.DMA((copies,)),

time: 31.3 us -> 29.6 us (0.946)
  Pallas kernels: 29.9 us -> 28.4 us
    pallas_call x1, Pallas kernels: 29.9 us -> 28.4 us  [body(): pl.pallas_call(kernel, out_shape=jax.ShapeDtypeStruct((ROWS, LEV * COLS),...]
where the time goes in v3:
time: 29.6 us; the launch traced here: 29.5 us
  Pallas kernels  28.4 us (96%)
  local copies, waits for them, and re-layouts  1.06 us (4%)
    pallas_call x1, Pallas kernels, body(): pl.pallas_call(kernel, out_shape=jax.ShapeDtypeStruct((ROWS, LEV * COLS),...  28.4 us
    unnamed x1, local copies, waits for them, and re-layouts  1.06 us

profile of v3, /device:TPU:33, one launch (start us, length us, event | category | flops | bytes accessed | tf_op | source)
XLA Modules:
  0.0 29.5 jit_solution(10672951389411906983)
XLA Ops:
  0.0 28.4 %shard_map.64 = f32[320,1024]{1,0:T(8,128)S(1)} custom-call(s32[16]{0:T(128)} %inter_hbm.1, f32[320,1024]{1,0:T(8,128)} %bitcast.7, f32[64,1024]{1,0:T(8,128)} %bitcast.8, bf16[320,320]{1,0:T(8,128)(2,1)} %bitcast.9, f32[6,80,80]{2,1,0:T(8,128)} %bitcast.10, s32[1,256]{1,0:T(1,128)} %bitcast.11), custom_call_target="tpu_custom_call" | custom-call | tf_op jit(solution)/shard_map/pallas_call | solution.py:585
  28.4 1.1 %copy.8 = f32[1,1,1,320,1024]{4,3,2,1,0:T(8,128)} copy(f32[1,1,1,320,1024]{4,3,2,1,0:T(8,128)S(1)} %bitcast.6) | data formatting | bytes 2621440

commit v4 on v3

--- a/solution.py
+++ b/solution.py
@@ -60,7 +60,7 @@
 
 def placement(face):
     row = iota((ROWS, FACE), 0)
-    col = iota((ROWS, FACE), 1)
+    col = iota((1, FACE), 1)
     field, first, second = col // 16, col // 4 % 4, col % 4
     pos = 3 * (face % 2)
     if face // 2 == 0:
@@ -237,7 +237,10 @@
     swap_face = remote(face_out, face_in, mates[0][2])
     copies1 = [remote(s1.at[q], r1.at[q], phase1[q]) for q in range(4)]
     copies2 = [remote(s2.at[d], r2.at[zf, d], dev) for zf, d, dev in phase2]
-    uas = [remote(ua_out.at[d], ua_in.at[zf, d], dev) for zf, d, dev in mates]
+    uas = [
+        remote(ua_out.at[d, pl.ds(0, 40 if d else 48)], ua_in.at[zf, d, pl.ds(0, 40 if d else 48)], dev)
+        for zf, d, dev in mates
+    ]
     ubs = [remote(ub_out.at[d], ub_in.at[d], place(c, z, x + d)) for d in range(1, 4)]
     patches = [remote(patch_out, patch_in.at[zf, d], dev) for zf, d, dev in mates]
     around = [
@@ -292,7 +295,7 @@
             copy.wait_recv()
         for d in range(4):
             s2[d] = r1[(8 - d - shift) % 4]
-        for copy in copies2:
+        for copy in copies2[3:] + copies2[:3]:
             copy.start()
         r2[0, 0] = s2[0]
 
@@ -407,8 +410,11 @@
         first(surface)
         held = surface_trace(w)
         pack_block(held, ua_out)
-        for q in range(4):
-            ua_out[q, 40:48] = jnp.broadcast_to(mask[:, 128 * (q // 2) : 128 * (q // 2) + 128], (8, 128))
+        ua_out[0, 40:48] = jnp.where(
+            iota((8, 128), 0) == 0,
+            jnp.broadcast_to(mask[:, 0:128], (8, 128)),
+            jnp.broadcast_to(mask[:, 128:256], (8, 128)),
+        )
 
     pl.semaphore_wait(
         barrier, 15 + jnp.where(y < last_y, 1, 0) + jnp.where(y > 0, 1, 0)
@@ -420,7 +426,7 @@
 
     prepare()
 
-    for copy in uas + [swap_face]:
+    for copy in uas[4:] + uas[:4] + [swap_face]:
         copy.start()
 
     def others(step):
@@ -502,7 +508,7 @@
     for copy in ubs + patches:
         copy.wait_recv()
     q = [ub_in[(8 - i - shift) % 4] for i in range(4)]
-    wet = jnp.concatenate([q[0][40:41], q[2][40:41]], axis=1)
+    wet = jnp.concatenate([q[0][40:41], q[0][41:42]], axis=1)
     patch = patch_in[z_pick, (4 - shift) % 4]
     tiles = [pltpu.roll(patch[0:8], (128 - 16 * r) % 128, 1) for r in range(5)]
     tiles += [pltpu.roll(patch[8:16], (128 - 2 * r) % 128, 1) for r in range(5)]
@@ -510,10 +516,10 @@
     high = packed.astype(BF16)
     low = (packed - high.astype(F32)).astype(BF16)
     row = iota((2 * FACE, FACE), 0)
-    col = iota((2 * FACE, FACE), 1)
-    node, face, index = row % FACE, col // 20, col % 20
+    col = iota((1, FACE), 1)
+    face, index = col // 20, col % 20
     target = index // 4 * 16 + jnp.where(face < 2, index % 4 + 12 * face, index % 4 * 4 + 3 * (face - 2))
-    to_node = ((node == target) & (row // FACE == face // 2)).astype(BF16)
+    to_node = (row == target + FACE * (face // 2)).astype(BF16)
     spread = jnp.dot(to_node, high, preferred_element_type=F32) + jnp.dot(
         to_node, low, preferred_element_type=F32
     )
@@ -539,11 +545,9 @@
             copy.wait_recv()
         partner = (g + (7 if k == 0 else 1) + delta) % 8
         row = iota((FACE, FACE), 0)
-        col = iota((FACE, FACE), 1)
-        pick = (
-            (row // 16 == col // 16) & (row % 4 == 3 * c) & (col % 4 == row // 4 % 4)
-            & (col // 4 % 4 == (3 if k == 0 else 0))
-        ).astype(BF16)
+        col = iota((1, FACE), 1)
+        target = jnp.where(col // 4 % 4 == (3 if k == 0 else 0), col // 16 * 16 + col % 4 * 4 + 3 * c, -1)
+        pick = (row == target).astype(BF16)
         op = jnp.dot(pick, small[4 + c], preferred_element_type=F32).astype(BF16)
         term = jnp.dot(op, split3(unfold_x(side_in[partner])), preferred_element_type=F32)
         held = pltpu.roll(unfold_half(rim_in[1, k, 0:40], 64), (128 - 48 * c) % 128, 1)

time: 29.6 us -> 28.7 us (0.970)
  Pallas kernels: 28.4 us -> 27.6 us
    pallas_call x1, Pallas kernels: 28.4 us -> 27.6 us  [body(): pl.pallas_call(kernel, out_shape=jax.ShapeDtypeStruct((ROWS, LEV * COLS),...]
where the time goes in v4:
time: 28.7 us; the launch traced here: 28.6 us
  Pallas kernels  27.6 us (96%)
  local copies, waits for them, and re-layouts  1.06 us (4%)
    pallas_call x1, Pallas kernels, body(): pl.pallas_call(kernel, out_shape=jax.ShapeDtypeStruct((ROWS, LEV * COLS),...  27.6 us
    unnamed x1, local copies, waits for them, and re-layouts  1.06 us

profile of v4, /device:TPU:33, one launch (start us, length us, event | category | flops | bytes accessed | tf_op | source)
XLA Modules:
  0.0 28.6 jit_solution(4452175290486483824)
XLA Ops:
  0.0 27.6 %shard_map.64 = f32[320,1024]{1,0:T(8,128)S(1)} custom-call(s32[16]{0:T(128)} %inter_hbm.1, f32[320,1024]{1,0:T(8,128)} %bitcast.7, f32[64,1024]{1,0:T(8,128)} %bitcast.8, bf16[320,320]{1,0:T(8,128)(2,1)} %bitcast.9, f32[6,80,80]{2,1,0:T(8,128)} %bitcast.10, s32[1,256]{1,0:T(1,128)} %bitcast.11), custom_call_target="tpu_custom_call" | custom-call | tf_op jit(solution)/shard_map/pallas_call | solution.py:589
  27.6 1.1 %copy.8 = f32[1,1,1,320,1024]{4,3,2,1,0:T(8,128)} copy(f32[1,1,1,320,1024]{4,3,2,1,0:T(8,128)S(1)} %bitcast.6) | data formatting | bytes 2621440
